TPU v7x, 512 devices: a whole 4x4x16 slice. The times are simulated.
512 devices in a mesh: seq: 64 (over y_lo, z, core), head: 8 (over x, y_hi).
Axes of the slice: x: 4, y: 4 (y_hi: 2, y_lo: 2; y = y_hi * 2 + y_lo), z: 16, core: 2. Of those that a mesh axis runs over, the one named last changes fastest.
Arguments:
- query_main: bfloat16 [8192, 2048], P(('seq', 'head')), may hold values from -5 to 5
- key_main: bfloat16 [8192, 2048], P(('seq', 'head')), may hold values from -5 to 5
- value_main: bfloat16 [8192, 2048], P(('seq', 'head')), may hold values from -5 to 5
- query_tan: bfloat16 [8192, 2048], P(('seq', 'head')), may hold values from -5 to 5
- key_tan: bfloat16 [8192, 2048], P(('seq', 'head')), may hold values from -5 to 5
- value_tan: bfloat16 [8192, 2048], P(('seq', 'head')), may hold values from -5 to 5
- positions: int32 [8192], P(('seq', 'head')), may hold values from 0 to 1073741823, as said below
Outputs:
- attended: bfloat16 [8192, 2048], P(('seq', 'head'))
- attended_tan: bfloat16 [8192, 2048], P(('seq', 'head'))
Inputs may be any that keep to these rules, and one draw needn't show every extreme that they name: `positions`: 8192 distinct values.
All inputs are finite; a program needn't handle non-finite values.
Results may differ from a plain program's by a relative error of at most 0.035.
Values may be sent and summed in bfloat16 or wider, within the bound.
A program may use at most 128 MiB of HBM per device.

v0:
```python
import jax
import jax.numpy as jnp
from jax import lax
from jax.sharding import PartitionSpec as P

HEAD_DIM = 128


def from_behind(value, axis, by):
    peers = lax.axis_size(axis)
    return lax.ppermute(value, axis, [(i, (i + by) % peers) for i in range(peers)])


def absorb(state, queries, query_dot, query_order, block, block_order):
    running_max, total, tangent_mass, value_sum, tangent_sum = state
    scale = HEAD_DIM ** (-0.5)
    keys = block[0]
    values = block[1]
    key_dot = block[2]
    value_dot = block[3]
    scores = jnp.einsum("qhd,khd->hqk", queries, keys, preferred_element_type=jnp.float32) * scale
    score_tan = (
        jnp.einsum("qhd,khd->hqk", query_dot, keys, preferred_element_type=jnp.float32)
        + jnp.einsum("qhd,khd->hqk", queries, key_dot, preferred_element_type=jnp.float32)
    ) * scale
    visible = block_order[None, :] <= query_order[:, None]
    scores = jnp.where(visible[None], scores, -1e30)
    new_max = jnp.maximum(running_max, jnp.max(scores, axis=-1))
    shrink = jnp.exp(running_max - new_max)
    expo = jnp.exp(scores - new_max[..., None])
    weighted = expo * score_tan
    total = total * shrink + jnp.sum(expo, axis=-1)
    tangent_mass = tangent_mass * shrink + jnp.sum(weighted, axis=-1)
    expo_low = expo.astype(jnp.bfloat16)
    weighted_low = weighted.astype(jnp.bfloat16)
    value_sum = value_sum * shrink[..., None] + jnp.einsum(
        "hqk,khd->hqd", expo_low, values, preferred_element_type=jnp.float32
    )
    tangent_sum = (
        tangent_sum * shrink[..., None]
        + jnp.einsum("hqk,khd->hqd", weighted_low, values, preferred_element_type=jnp.float32)
        + jnp.einsum("hqk,khd->hqd", expo_low, value_dot, preferred_element_type=jnp.float32)
    )
    return (new_max, total, tangent_mass, value_sum, tangent_sum)


def local(query_main, key_main, value_main, query_tan, key_tan, value_tan, positions):
    all_positions = lax.all_gather(positions, ("seq", "head"), axis=0, tiled=True)
    moved = (
        lax.all_to_all(query_main, "head", split_axis=1, concat_axis=0, tiled=True),
        lax.all_to_all(key_main, "head", split_axis=1, concat_axis=0, tiled=True),
        lax.all_to_all(value_main, "head", split_axis=1, concat_axis=0, tiled=True),
        lax.all_to_all(query_tan, "head", split_axis=1, concat_axis=0, tiled=True),
        lax.all_to_all(key_tan, "head", split_axis=1, concat_axis=0, tiled=True),
        lax.all_to_all(value_tan, "head", split_axis=1, concat_axis=0, tiled=True),
    )
    rows_here = moved[0].shape[0]
    heads_here = moved[0].shape[1] // HEAD_DIM
    shaped = [piece.reshape(rows_here, heads_here, HEAD_DIM) for piece in moved]
    queries, keys, values, query_dot, key_dot, value_dot = shaped
    count = lax.axis_size("seq")
    place = lax.axis_index("seq")
    own_order = lax.dynamic_slice_in_dim(all_positions, place * rows_here, rows_here)
    stacked = jnp.stack([keys, values, key_dot, value_dot])
    state = (
        jnp.full((heads_here, rows_here), -1e30, jnp.float32),
        jnp.zeros((heads_here, rows_here), jnp.float32),
        jnp.zeros((heads_here, rows_here), jnp.float32),
        jnp.zeros((heads_here, rows_here, HEAD_DIM), jnp.float32),
        jnp.zeros((heads_here, rows_here, HEAD_DIM), jnp.float32),
    )
    state = absorb(state, queries, query_dot, own_order, stacked, own_order)

    def advance(step, carry):
        travelling, current = carry
        travelling = from_behind(travelling, "seq", 1)
        source = (place - step) % count
        order = lax.dynamic_slice_in_dim(all_positions, source * rows_here, rows_here)
        return (travelling, absorb(current, queries, query_dot, own_order, travelling, order))

    travelling, state = lax.fori_loop(1, count, advance, (stacked, state))
    running_max, total, tangent_mass, value_sum, tangent_sum = state
    output = value_sum / total[..., None]
    weight = tangent_mass / total
    tangent_out = tangent_sum / total[..., None] - weight[..., None] * output
    output_low = (
        jnp.transpose(output, (1, 0, 2))
        .reshape(rows_here, heads_here * HEAD_DIM)
        .astype(jnp.bfloat16)
    )
    tangent_low = (
        jnp.transpose(tangent_out, (1, 0, 2))
        .reshape(rows_here, heads_here * HEAD_DIM)
        .astype(jnp.bfloat16)
    )
    returned = (
        lax.all_to_all(output_low, "head", split_axis=0, concat_axis=1, tiled=True),
        lax.all_to_all(tangent_low, "head", split_axis=0, concat_axis=1, tiled=True),
    )
    return (returned[0], returned[1])


def solution(mesh):
    placed = (
        P(("seq", "head"), None),
        P(("seq", "head"), None),
        P(("seq", "head"), None),
        P(("seq", "head"), None),
        P(("seq", "head"), None),
        P(("seq", "head"), None),
        P(("seq", "head")),
    )
    return jax.shard_map(
        local,
        mesh=mesh,
        in_specs=placed,
        out_specs=(P(("seq", "head"), None), P(("seq", "head"), None)),
        check_vma=False,
    )
```

profile of v0, /device:TPU:2, one launch (start us, length us, event | category | flops | bytes accessed | tf_op | source)
XLA Modules:
  0.0 907.3 jit_solution(3921272314341392415)
XLA Ops:
  2.1 9.3 %all-to-all-start.4 = ((bf16[16,8,256]{2,0,1:T(8,128)(2,1)}), bf16[16,8,256]{2,0,1:T(8,128)(2,1)S(1)}, u32[]{:S(2)}, u32[]{:S(2)}) async-start(bf16[16,8,256]{2,0,1:T(8,128)(2,1)} %bitcast.58), calls=%async_computation.4 | async-start | bytes 131072 | tf_op jit(solution)/shard_map/all_to_all | solution.py:50
  57.6 106.3 %all-reduce = s32[8192]{0:T(1024)S(1)} all-reduce(s32[8192]{0:T(1024)S(1)} %dynamic-update-slice), channel_id=1, replica_groups=mesh['seq'=64,'head'=8] {'seq','head'}, use_global_device_ids=true, to_apply=%add | all-reduce | flops 8192 | bytes 65536
  176.9 706.7 %while.25 = (s32[]{:T(128)}, bf16[4,128,2,128]{3,1,2,0:T(8,128)(2,1)S(1)}, f32[2,128]{1,0:T(2,128)S(1)}, f32[2,128]{1,0:T(2,128)S(1)}, f32[2,128]{1,0:T(2,128)S(...) while((s32[]{:T(128)}, ...), condition=%wide.region_7.8_spmd, body=%wide.region_3.7_spmd.sunk | while | flops 51004176 | bytes 4057464 | solution.py:81
  179.1 7.7 collective-permute-done
  235.2 7.7 collective-permute-done
  246.4 7.7 collective-permute-done
  257.6 7.7 collective-permute-done
  268.8 7.7 collective-permute-done
  280.0 7.7 collective-permute-done
  347.3 7.7 collective-permute-done
  358.5 7.7 collective-permute-done
  369.8 7.7 collective-permute-done
  381.0 7.7 collective-permute-done
  448.3 7.7 collective-permute-done
  459.5 7.7 collective-permute-done
  470.7 7.7 collective-permute-done
  481.9 7.7 collective-permute-done
  493.1 7.7 collective-permute-done
  560.4 7.7 collective-permute-done
  571.7 7.7 collective-permute-done
  582.9 7.7 collective-permute-done
  594.1 7.7 collective-permute-done
  661.4 7.7 collective-permute-done
  672.6 7.7 collective-permute-done
  683.8 7.7 collective-permute-done
  695.1 7.7 collective-permute-done
  706.3 7.7 collective-permute-done
  773.6 7.7 collective-permute-done
  784.8 7.7 collective-permute-done
  796.0 7.7 collective-permute-done
  807.2 7.7 collective-permute-done
  874.5 7.7 collective-permute-done
  (1047 shorter events, 561.7 us)
Async XLA Ops:
  2.1 15.6 %all-to-all-start.4 = ((bf16[16,8,256]{2,0,1:T(8,128)(2,1)}), bf16[16,8,256]{2,0,1:T(8,128)(2,1)S(1)}, u32[]{:S(2)}, u32[]{:S(2)}) async-start(bf16[16,8,256]{2,0,1:T(8,128)(2,1)} %bitcast.58), calls=%async_computation.4 | async-start | bytes 131072 | tf_op jit(solution)/shard_map/all_to_all | solution.py:50
  17.7 11.2 %all-to-all-start = ((bf16[16,8,256]{2,0,1:T(8,128)(2,1)}), bf16[16,8,256]{2,0,1:T(8,128)(2,1)S(1)}, u32[]{:S(2)}, u32[]{:S(2)}) async-start(bf16[16,8,256]{2,0,1:T(8,128)(2,1)} %bitcast.62), calls=%async_computation | async-start | bytes 131072 | tf_op jit(solution)/shard_map/all_to_all | solution.py:51
  28.9 11.2 %all-to-all-start.1 = ((bf16[16,8,256]{2,0,1:T(8,128)(2,1)}), bf16[16,8,256]{2,0,1:T(8,128)(2,1)S(1)}, u32[]{:S(2)}, u32[]{:S(2)}) async-start(bf16[16,8,256]{2,0,1:T(8,128)(2,1)} %bitcast.61), calls=%async_computation.1 | async-start | bytes 131072 | tf_op jit(solution)/shard_map/all_to_all | solution.py:52
  40.1 11.2 %all-to-all-start.2 = ((bf16[16,8,256]{2,0,1:T(8,128)(2,1)}), bf16[16,8,256]{2,0,1:T(8,128)(2,1)S(1)}, u32[]{:S(2)}, u32[]{:S(2)}) async-start(bf16[16,8,256]{2,0,1:T(8,128)(2,1)} %bitcast.60), calls=%async_computation.2 | async-start | bytes 131072 | tf_op jit(solution)/shard_map/all_to_all | solution.py:54
  51.3 112.7 %all-to-all-start.3 = ((bf16[16,8,256]{2,0,1:T(8,128)(2,1)}), bf16[16,8,256]{2,0,1:T(8,128)(2,1)S(1)}, u32[]{:S(2)}, u32[]{:S(2)}) async-start(bf16[16,8,256]{2,0,1:T(8,128)(2,1)} %bitcast.59), calls=%async_computation.3 | async-start | bytes 131072 | tf_op jit(solution)/shard_map/all_to_all | solution.py:55
  164.0 11.1 %all-to-all-start.5 = ((bf16[16,8,256]{2,0,1:T(8,128)(2,1)}), bf16[16,8,256]{2,0,1:T(8,128)(2,1)S(1)}, u32[]{:S(2)}, u32[]{:S(2)}) async-start(bf16[16,8,256]{2,0,1:T(8,128)(2,1)} %bitcast.57), calls=%async_computation.5 | async-start | bytes 131072 | tf_op jit(solution)/shard_map/all_to_all | solution.py:53
  177.0 9.8 %collective-permute-start = (bf16[4,128,2,128]{3,1,2,0:T(8,128)(2,1)S(1)}, bf16[4,128,2,128]{3,1,2,0:T(8,128)(2,1)S(1)}, u32[]{:S(2)}, u32[]{:S(2)}) collective-permute-start(bf16[4,128,2,128]{3,1,2,0:T(8,128)(2,1)S(1)} %get-tuple-element.467), channel_id=1, source_target_pairs={{0,8},{8,16},{16,24},{24,32},{32,40},{40,48},{48,56},{56,64},{64,7... | collective-permute-start | bytes 786440 | tf_op jit(solution)/shard_map/while/body/eval_jaxpr/ppermute | solution.py:11
  188.2 9.8 %collective-permute-start = (bf16[4,128,2,128]{3,1,2,0:T(8,128)(2,1)S(1)}, bf16[4,128,2,128]{3,1,2,0:T(8,128)(2,1)S(1)}, u32[]{:S(2)}, u32[]{:S(2)}) collective-permute-start(bf16[4,128,2,128]{3,1,2,0:T(8,128)(2,1)S(1)} %get-tuple-element.467), channel_id=1, source_target_pairs={{0,8},{8,16},{16,24},{24,32},{32,40},{40,48},{48,56},{56,64},{64,7... | collective-permute-start | bytes 786440 | tf_op jit(solution)/shard_map/while/body/eval_jaxpr/ppermute | solution.py:11
  199.4 9.8 %collective-permute-start = (bf16[4,128,2,128]{3,1,2,0:T(8,128)(2,1)S(1)}, bf16[4,128,2,128]{3,1,2,0:T(8,128)(2,1)S(1)}, u32[]{:S(2)}, u32[]{:S(2)}) collective-permute-start(bf16[4,128,2,128]{3,1,2,0:T(8,128)(2,1)S(1)} %get-tuple-element.467), channel_id=1, source_target_pairs={{0,8},{8,16},{16,24},{24,32},{32,40},{40,48},{48,56},{56,64},{64,7... | collective-permute-start | bytes 786440 | tf_op jit(solution)/shard_map/while/body/eval_jaxpr/ppermute | solution.py:11
  210.6 9.8 %collective-permute-start = (bf16[4,128,2,128]{3,1,2,0:T(8,128)(2,1)S(1)}, bf16[4,128,2,128]{3,1,2,0:T(8,128)(2,1)S(1)}, u32[]{:S(2)}, u32[]{:S(2)}) collective-permute-start(bf16[4,128,2,128]{3,1,2,0:T(8,128)(2,1)S(1)} %get-tuple-element.467), channel_id=1, source_target_pairs={{0,8},{8,16},{16,24},{24,32},{32,40},{40,48},{48,56},{56,64},{64,7... | collective-permute-start | bytes 786440 | tf_op jit(solution)/shard_map/while/body/eval_jaxpr/ppermute | solution.py:11
  221.8 9.8 %collective-permute-start = (bf16[4,128,2,128]{3,1,2,0:T(8,128)(2,1)S(1)}, bf16[4,128,2,128]{3,1,2,0:T(8,128)(2,1)S(1)}, u32[]{:S(2)}, u32[]{:S(2)}) collective-permute-start(bf16[4,128,2,128]{3,1,2,0:T(8,128)(2,1)S(1)} %get-tuple-element.467), channel_id=1, source_target_pairs={{0,8},{8,16},{16,24},{24,32},{32,40},{40,48},{48,56},{56,64},{64,7... | collective-permute-start | bytes 786440 | tf_op jit(solution)/shard_map/while/body/eval_jaxpr/ppermute | solution.py:11
  233.0 9.8 %collective-permute-start = (bf16[4,128,2,128]{3,1,2,0:T(8,128)(2,1)S(1)}, bf16[4,128,2,128]{3,1,2,0:T(8,128)(2,1)S(1)}, u32[]{:S(2)}, u32[]{:S(2)}) collective-permute-start(bf16[4,128,2,128]{3,1,2,0:T(8,128)(2,1)S(1)} %get-tuple-element.467), channel_id=1, source_target_pairs={{0,8},{8,16},{16,24},{24,32},{32,40},{40,48},{48,56},{56,64},{64,7... | collective-permute-start | bytes 786440 | tf_op jit(solution)/shard_map/while/body/eval_jaxpr/ppermute | solution.py:11
  244.3 9.8 %collective-permute-start = (bf16[4,128,2,128]{3,1,2,0:T(8,128)(2,1)S(1)}, bf16[4,128,2,128]{3,1,2,0:T(8,128)(2,1)S(1)}, u32[]{:S(2)}, u32[]{:S(2)}) collective-permute-start(bf16[4,128,2,128]{3,1,2,0:T(8,128)(2,1)S(1)} %get-tuple-element.467), channel_id=1, source_target_pairs={{0,8},{8,16},{16,24},{24,32},{32,40},{40,48},{48,56},{56,64},{64,7... | collective-permute-start | bytes 786440 | tf_op jit(solution)/shard_map/while/body/eval_jaxpr/ppermute | solution.py:11
  255.5 9.8 %collective-permute-start = (bf16[4,128,2,128]{3,1,2,0:T(8,128)(2,1)S(1)}, bf16[4,128,2,128]{3,1,2,0:T(8,128)(2,1)S(1)}, u32[]{:S(2)}, u32[]{:S(2)}) collective-permute-start(bf16[4,128,2,128]{3,1,2,0:T(8,128)(2,1)S(1)} %get-tuple-element.467), channel_id=1, source_target_pairs={{0,8},{8,16},{16,24},{24,32},{32,40},{40,48},{48,56},{56,64},{64,7... | collective-permute-start | bytes 786440 | tf_op jit(solution)/shard_map/while/body/eval_jaxpr/ppermute | solution.py:11
  345.2 9.8 %collective-permute-start = (bf16[4,128,2,128]{3,1,2,0:T(8,128)(2,1)S(1)}, bf16[4,128,2,128]{3,1,2,0:T(8,128)(2,1)S(1)}, u32[]{:S(2)}, u32[]{:S(2)}) collective-permute-start(bf16[4,128,2,128]{3,1,2,0:T(8,128)(2,1)S(1)} %get-tuple-element.467), channel_id=1, source_target_pairs={{0,8},{8,16},{16,24},{24,32},{32,40},{40,48},{48,56},{56,64},{64,7... | collective-permute-start | bytes 786440 | tf_op jit(solution)/shard_map/while/body/eval_jaxpr/ppermute | solution.py:11
  356.4 9.8 %collective-permute-start = (bf16[4,128,2,128]{3,1,2,0:T(8,128)(2,1)S(1)}, bf16[4,128,2,128]{3,1,2,0:T(8,128)(2,1)S(1)}, u32[]{:S(2)}, u32[]{:S(2)}) collective-permute-start(bf16[4,128,2,128]{3,1,2,0:T(8,128)(2,1)S(1)} %get-tuple-element.467), channel_id=1, source_target_pairs={{0,8},{8,16},{16,24},{24,32},{32,40},{40,48},{48,56},{56,64},{64,7... | collective-permute-start | bytes 786440 | tf_op jit(solution)/shard_map/while/body/eval_jaxpr/ppermute | solution.py:11
  367.6 9.8 %collective-permute-start = (bf16[4,128,2,128]{3,1,2,0:T(8,128)(2,1)S(1)}, bf16[4,128,2,128]{3,1,2,0:T(8,128)(2,1)S(1)}, u32[]{:S(2)}, u32[]{:S(2)}) collective-permute-start(bf16[4,128,2,128]{3,1,2,0:T(8,128)(2,1)S(1)} %get-tuple-element.467), channel_id=1, source_target_pairs={{0,8},{8,16},{16,24},{24,32},{32,40},{40,48},{48,56},{56,64},{64,7... | collective-permute-start | bytes 786440 | tf_op jit(solution)/shard_map/while/body/eval_jaxpr/ppermute | solution.py:11
  446.2 9.8 %collective-permute-start = (bf16[4,128,2,128]{3,1,2,0:T(8,128)(2,1)S(1)}, bf16[4,128,2,128]{3,1,2,0:T(8,128)(2,1)S(1)}, u32[]{:S(2)}, u32[]{:S(2)}) collective-permute-start(bf16[4,128,2,128]{3,1,2,0:T(8,128)(2,1)S(1)} %get-tuple-element.467), channel_id=1, source_target_pairs={{0,8},{8,16},{16,24},{24,32},{32,40},{40,48},{48,56},{56,64},{64,7... | collective-permute-start | bytes 786440 | tf_op jit(solution)/shard_map/while/body/eval_jaxpr/ppermute | solution.py:11
  457.4 9.8 %collective-permute-start = (bf16[4,128,2,128]{3,1,2,0:T(8,128)(2,1)S(1)}, bf16[4,128,2,128]{3,1,2,0:T(8,128)(2,1)S(1)}, u32[]{:S(2)}, u32[]{:S(2)}) collective-permute-start(bf16[4,128,2,128]{3,1,2,0:T(8,128)(2,1)S(1)} %get-tuple-element.467), channel_id=1, source_target_pairs={{0,8},{8,16},{16,24},{24,32},{32,40},{40,48},{48,56},{56,64},{64,7... | collective-permute-start | bytes 786440 | tf_op jit(solution)/shard_map/while/body/eval_jaxpr/ppermute | solution.py:11
  468.6 9.8 %collective-permute-start = (bf16[4,128,2,128]{3,1,2,0:T(8,128)(2,1)S(1)}, bf16[4,128,2,128]{3,1,2,0:T(8,128)(2,1)S(1)}, u32[]{:S(2)}, u32[]{:S(2)}) collective-permute-start(bf16[4,128,2,128]{3,1,2,0:T(8,128)(2,1)S(1)} %get-tuple-element.467), channel_id=1, source_target_pairs={{0,8},{8,16},{16,24},{24,32},{32,40},{40,48},{48,56},{56,64},{64,7... | collective-permute-start | bytes 786440 | tf_op jit(solution)/shard_map/while/body/eval_jaxpr/ppermute | solution.py:11
  558.3 9.8 %collective-permute-start = (bf16[4,128,2,128]{3,1,2,0:T(8,128)(2,1)S(1)}, bf16[4,128,2,128]{3,1,2,0:T(8,128)(2,1)S(1)}, u32[]{:S(2)}, u32[]{:S(2)}) collective-permute-start(bf16[4,128,2,128]{3,1,2,0:T(8,128)(2,1)S(1)} %get-tuple-element.467), channel_id=1, source_target_pairs={{0,8},{8,16},{16,24},{24,32},{32,40},{40,48},{48,56},{56,64},{64,7... | collective-permute-start | bytes 786440 | tf_op jit(solution)/shard_map/while/body/eval_jaxpr/ppermute | solution.py:11
  569.5 9.8 %collective-permute-start = (bf16[4,128,2,128]{3,1,2,0:T(8,128)(2,1)S(1)}, bf16[4,128,2,128]{3,1,2,0:T(8,128)(2,1)S(1)}, u32[]{:S(2)}, u32[]{:S(2)}) collective-permute-start(bf16[4,128,2,128]{3,1,2,0:T(8,128)(2,1)S(1)} %get-tuple-element.467), channel_id=1, source_target_pairs={{0,8},{8,16},{16,24},{24,32},{32,40},{40,48},{48,56},{56,64},{64,7... | collective-permute-start | bytes 786440 | tf_op jit(solution)/shard_map/while/body/eval_jaxpr/ppermute | solution.py:11
  580.8 9.8 %collective-permute-start = (bf16[4,128,2,128]{3,1,2,0:T(8,128)(2,1)S(1)}, bf16[4,128,2,128]{3,1,2,0:T(8,128)(2,1)S(1)}, u32[]{:S(2)}, u32[]{:S(2)}) collective-permute-start(bf16[4,128,2,128]{3,1,2,0:T(8,128)(2,1)S(1)} %get-tuple-element.467), channel_id=1, source_target_pairs={{0,8},{8,16},{16,24},{24,32},{32,40},{40,48},{48,56},{56,64},{64,7... | collective-permute-start | bytes 786440 | tf_op jit(solution)/shard_map/while/body/eval_jaxpr/ppermute | solution.py:11
  659.3 9.8 %collective-permute-start = (bf16[4,128,2,128]{3,1,2,0:T(8,128)(2,1)S(1)}, bf16[4,128,2,128]{3,1,2,0:T(8,128)(2,1)S(1)}, u32[]{:S(2)}, u32[]{:S(2)}) collective-permute-start(bf16[4,128,2,128]{3,1,2,0:T(8,128)(2,1)S(1)} %get-tuple-element.467), channel_id=1, source_target_pairs={{0,8},{8,16},{16,24},{24,32},{32,40},{40,48},{48,56},{56,64},{64,7... | collective-permute-start | bytes 786440 | tf_op jit(solution)/shard_map/while/body/eval_jaxpr/ppermute | solution.py:11
  670.5 9.8 %collective-permute-start = (bf16[4,128,2,128]{3,1,2,0:T(8,128)(2,1)S(1)}, bf16[4,128,2,128]{3,1,2,0:T(8,128)(2,1)S(1)}, u32[]{:S(2)}, u32[]{:S(2)}) collective-permute-start(bf16[4,128,2,128]{3,1,2,0:T(8,128)(2,1)S(1)} %get-tuple-element.467), channel_id=1, source_target_pairs={{0,8},{8,16},{16,24},{24,32},{32,40},{40,48},{48,56},{56,64},{64,7... | collective-permute-start | bytes 786440 | tf_op jit(solution)/shard_map/while/body/eval_jaxpr/ppermute | solution.py:11
  681.7 9.8 %collective-permute-start = (bf16[4,128,2,128]{3,1,2,0:T(8,128)(2,1)S(1)}, bf16[4,128,2,128]{3,1,2,0:T(8,128)(2,1)S(1)}, u32[]{:S(2)}, u32[]{:S(2)}) collective-permute-start(bf16[4,128,2,128]{3,1,2,0:T(8,128)(2,1)S(1)} %get-tuple-element.467), channel_id=1, source_target_pairs={{0,8},{8,16},{16,24},{24,32},{32,40},{40,48},{48,56},{56,64},{64,7... | collective-permute-start | bytes 786440 | tf_op jit(solution)/shard_map/while/body/eval_jaxpr/ppermute | solution.py:11
  771.4 9.8 %collective-permute-start = (bf16[4,128,2,128]{3,1,2,0:T(8,128)(2,1)S(1)}, bf16[4,128,2,128]{3,1,2,0:T(8,128)(2,1)S(1)}, u32[]{:S(2)}, u32[]{:S(2)}) collective-permute-start(bf16[4,128,2,128]{3,1,2,0:T(8,128)(2,1)S(1)} %get-tuple-element.467), channel_id=1, source_target_pairs={{0,8},{8,16},{16,24},{24,32},{32,40},{40,48},{48,56},{56,64},{64,7... | collective-permute-start | bytes 786440 | tf_op jit(solution)/shard_map/while/body/eval_jaxpr/ppermute | solution.py:11
  782.7 9.8 %collective-permute-start = (bf16[4,128,2,128]{3,1,2,0:T(8,128)(2,1)S(1)}, bf16[4,128,2,128]{3,1,2,0:T(8,128)(2,1)S(1)}, u32[]{:S(2)}, u32[]{:S(2)}) collective-permute-start(bf16[4,128,2,128]{3,1,2,0:T(8,128)(2,1)S(1)} %get-tuple-element.467), channel_id=1, source_target_pairs={{0,8},{8,16},{16,24},{24,32},{32,40},{40,48},{48,56},{56,64},{64,7... | collective-permute-start | bytes 786440 | tf_op jit(solution)/shard_map/while/body/eval_jaxpr/ppermute | solution.py:11
  793.9 9.8 %collective-permute-start = (bf16[4,128,2,128]{3,1,2,0:T(8,128)(2,1)S(1)}, bf16[4,128,2,128]{3,1,2,0:T(8,128)(2,1)S(1)}, u32[]{:S(2)}, u32[]{:S(2)}) collective-permute-start(bf16[4,128,2,128]{3,1,2,0:T(8,128)(2,1)S(1)} %get-tuple-element.467), channel_id=1, source_target_pairs={{0,8},{8,16},{16,24},{24,32},{32,40},{40,48},{48,56},{56,64},{64,7... | collective-permute-start | bytes 786440 | tf_op jit(solution)/shard_map/while/body/eval_jaxpr/ppermute | solution.py:11
  872.4 9.8 %collective-permute-start = (bf16[4,128,2,128]{3,1,2,0:T(8,128)(2,1)S(1)}, bf16[4,128,2,128]{3,1,2,0:T(8,128)(2,1)S(1)}, u32[]{:S(2)}, u32[]{:S(2)}) collective-permute-start(bf16[4,128,2,128]{3,1,2,0:T(8,128)(2,1)S(1)} %get-tuple-element.467), channel_id=1, source_target_pairs={{0,8},{8,16},{16,24},{24,32},{32,40},{40,48},{48,56},{56,64},{64,7... | collective-permute-start | bytes 786440 | tf_op jit(solution)/shard_map/while/body/eval_jaxpr/ppermute | solution.py:11
  884.5 11.1 %all-to-all-start.7 = ((bf16[8,16,256]{2,1,0:T(8,128)(2,1)}), bf16[8,16,256]{2,1,0:T(8,128)(2,1)S(1)}, u32[]{:S(2)}, u32[]{:S(2)}) async-start(bf16[8,16,256]{2,1,0:T(8,128)(2,1)} %convert_element_type.53), calls=%async_computation.7 | async-start | bytes 131072 | tf_op jit(solution)/shard_map/all_to_all | solution.py:98
  895.6 11.0 %all-to-all-start.6 = ((bf16[8,16,256]{2,1,0:T(8,128)(2,1)}), bf16[8,16,256]{2,1,0:T(8,128)(2,1)S(1)}, u32[]{:S(2)}, u32[]{:S(2)}) async-start(bf16[8,16,256]{2,1,0:T(8,128)(2,1)} %convert_element_type.50), calls=%async_computation.6 | async-start | bytes 131072 | tf_op jit(solution)/shard_map/all_to_all | solution.py:97
  (45 other events, 411.6 us)
where the time goes:
time: 913 us; the launch traced here: 907 us
  waiting for transfers between devices  524 us (57%)
  starting transfers between devices  164 us (18%)
  blocking collectives  106 us (12%)
  matrix products  79.9 us (9%)
  local copies, waits for them, and re-layouts  15.3 us (2%)
  other arithmetic  10.8 us (1%)
    ppermute x63, waiting for transfers between devices, from_behind(): lax.ppermute(value, axis, [(i, (i + by) % peers) for i in range(peers)])  484 us
    ppermute x63, starting transfers between devices, from_behind(): lax.ppermute(value, axis, [(i, (i + by) % peers) for i in range(peers)])  121 us
    unnamed x1, blocking collectives  106 us
  transfers between devices with their start and end apart: 71, of which 70 were waited for; matrix products, arithmetic and copies ran while one was open for 2% of the time, Pallas kernels for 0%

commit v1 on v0

v1 whole, which is shorter than its diff:
```python
import jax
import jax.numpy as jnp
from jax import lax
from jax.experimental import pallas as pl
from jax.experimental.pallas import tpu as pltpu
from jax.sharding import PartitionSpec as P

D = 128
NZ = 16
ROWS = 16
BLOCK = NZ * ROWS
KB = 8
QB = 4
SCALE = D ** -0.5
LOG2E = 1.4426950408889634
CHUNKS = 2
SLOTS = NZ // CHUNKS
CROWS = SLOTS * ROWS
NEG = -1e30
MESH = pl.DeviceIdType.MESH


def offset(i):
    return ((i + 1) // 2) * (2 * (i % 2) - 1)


def kernel(q_ref, k_ref, v_ref, dq_ref, dk_ref, dv_ref, pos_ref,
           out_ref, tan_ref,
           kpack, qpack, prow, kbuf, qbuf, pbuf, kpos, qpos,
           s_buf, p_buf, w_buf,
           part, pstat, opart, ostat, obuf, rbuf,
           zk_send, zk_recv, zq_send, zq_recv, zp_send, zp_recv,
           k_send, k_recv, q_send, q_recv, kp_send, kp_recv, qp_send, qp_recv,
           o_send, o_recv, st_send, st_recv, f_send, f_recv):
    s = lax.axis_index("seq")
    h = lax.axis_index("head")
    c = s % 2
    z = (s // 2) % NZ
    y = (h % 2) * 2 + s // (2 * NZ)
    x = h // 2

    def device(x_, y_, z_, c_):
        return (((y_ % 2) * NZ + z_) * 2 + c_, x_ * 2 + y_ // 2)

    def along_z(by):
        return device(x, y, (z + by + NZ) % NZ, c)

    def along_x(by):
        return device((x + by) % 4, y, z, c)

    def along_y(by):
        return device(x, (y + by) % 4, z, c)

    twin = device(x, y, z, 1 - c)

    barrier = pltpu.get_barrier_semaphore()

    def greet(i, carry):
        pl.semaphore_signal(barrier, inc=1, device_id=along_z(i), device_id_type=MESH)
        return carry

    lax.fori_loop(1, NZ, greet, 0)
    for by in (1, 2, 3):
        pl.semaphore_signal(barrier, inc=1, device_id=along_x(by), device_id_type=MESH)
        pl.semaphore_signal(barrier, inc=1, device_id=along_y(by), device_id_type=MESH)
        pl.semaphore_signal(barrier, inc=1, device_id=device((x + by) % 4, y, z, 1 - c), device_id_type=MESH)
    pl.semaphore_signal(barrier, inc=1, device_id=twin, device_id_type=MESH)

    for head in range(NZ):
        rows = pl.ds(head * ROWS, ROWS)
        cols = pl.ds(head * D, D)
        for at, ref in enumerate((k_ref, dk_ref, v_ref, dv_ref)):
            kpack[rows, at * D:(at + 1) * D] = ref[:, cols]
        for at, ref in enumerate((dq_ref, q_ref)):
            qpack[rows, at * D:(at + 1) * D] = ref[:, cols]
    lane = lax.broadcasted_iota(jnp.int32, (1, D), 1)
    row = jnp.zeros((1, D), jnp.int32)
    for i in range(ROWS):
        row = jnp.where(lane % ROWS == i, pos_ref[i], row)
    prow[...] = row

    pl.semaphore_wait(barrier, NZ - 1 + 10)

    def z_copies(i):
        by = offset(i)
        to = along_z(-by)
        source = pl.ds(pl.multiple_of(((z - by + NZ) % NZ) * ROWS, ROWS), ROWS)
        slot = pl.ds(pl.multiple_of(i * ROWS, ROWS), ROWS)
        return (
            pltpu.make_async_remote_copy(
                kpack.at[source, :], kbuf.at[0, slot, :], zk_send.at[i], zk_recv.at[i],
                device_id=to, device_id_type=MESH),
            pltpu.make_async_remote_copy(
                qpack.at[source, :], qbuf.at[0, slot, :], zq_send.at[i], zq_recv.at[i],
                device_id=to, device_id_type=MESH),
            pltpu.make_async_remote_copy(
                prow, pbuf.at[i], zp_send.at[i], zp_recv.at[i],
                device_id=to, device_id_type=MESH),
        )

    def z_start(i, carry):
        for copy in z_copies(i):
            copy.start()
        return carry

    lax.fori_loop(1, NZ, z_start, 0)
    own = pl.ds(pl.multiple_of(z * ROWS, ROWS), ROWS)
    kbuf[0, 0:ROWS, :] = kpack[own, :]
    qbuf[0, 0:ROWS, :] = qpack[own, :]
    pbuf[0] = prow[...]

    def k_copy(block, rows, to, at, sem):
        return pltpu.make_async_remote_copy(
            kbuf.at[block, rows, :], kbuf.at[at, rows, :], k_send.at[sem], k_recv.at[sem],
            device_id=to, device_id_type=MESH)

    def q_copy(block, rows, to, at, sem):
        return pltpu.make_async_remote_copy(
            qbuf.at[block, rows, :], qbuf.at[at, rows, :], q_send.at[sem], q_recv.at[sem],
            device_id=to, device_id_type=MESH)

    half = CROWS // 2

    def first_copies(g):
        rows = pl.ds(g * CROWS, CROWS)
        return (
            k_copy(0, rows, along_x(1), 6, g * 8 + 6),
            k_copy(0, rows, along_x(3), 2, g * 8 + 2),
            q_copy(0, rows, along_y(1), 3, g * 4 + 3),
            q_copy(0, rows, along_y(3), 1, g * 4 + 1),
            k_copy(0, rows, twin, 1, g * 8 + 1),
        )

    def second_copies(g):
        low = pl.ds(g * CROWS, half)
        high = pl.ds(g * CROWS + half, half)
        rows = pl.ds(g * CROWS, CROWS)
        return (
            k_copy(2, low, along_x(3), 4, g * 8 + 4),
            k_copy(6, high, along_x(1), 4, g * 8 + 0),
            q_copy(1, low, along_y(3), 2, g * 4 + 2),
            q_copy(3, high, along_y(1), 2, g * 4 + 0),
            k_copy(2, rows, twin, 3, g * 8 + 3),
            k_copy(6, rows, twin, 7, g * 8 + 7),
        )

    def third_copies(g):
        return (k_copy(4, pl.ds(g * CROWS, CROWS), twin, 5, g * 8 + 5),)

    def kp_copy(to, at):
        return pltpu.make_async_remote_copy(
            kpos.at[0], kpos.at[at], kp_send.at[at], kp_recv.at[at],
            device_id=to, device_id_type=MESH)

    def qp_copy(to, at):
        return pltpu.make_async_remote_copy(
            kpos.at[0], qpos.at[at], qp_send.at[at], qp_recv.at[at],
            device_id=to, device_id_type=MESH)

    def pos_copies():
        copies = [kp_copy(twin, 1)]
        for by in (1, 2, 3):
            copies.append(kp_copy(along_x(4 - by), 2 * by))
            copies.append(kp_copy(device((x + 4 - by) % 4, y, z, 1 - c), 2 * by + 1))
            copies.append(qp_copy(along_y(4 - by), by))
        return copies

    def stage_one(g):
        def arrive(i, carry):
            for copy in z_copies(i):
                copy.wait_recv()
            return carry

        lax.fori_loop(max(1, g * SLOTS), (g + 1) * SLOTS, arrive, 0)
        for copy in first_copies(g):
            copy.start()

    def stage_two(g):
        for copy in first_copies(g)[:4]:
            copy.wait_recv()
        for copy in second_copies(g):
            copy.start()

    def stage_three(g):
        for copy in second_copies(g)[:4]:
            copy.wait_recv()
        for copy in third_copies(g):
            copy.start()

    for step in range(CHUNKS + 2):
        if step < CHUNKS:
            stage_one(step)
        if step == CHUNKS - 1:
            total = []
            for g in range(2):
                line = jnp.zeros((1, D), jnp.int32)
                for i in range(8):
                    line = jnp.where(lane // ROWS == i, pbuf[g * 8 + i], line)
                total.append(line)
            line = jnp.concatenate(total, axis=1)
            kpos[0] = line
            qpos[0] = line
            for copy in pos_copies():
                copy.start()
        if 0 <= step - 1 < CHUNKS:
            stage_two(step - 1)
        if 0 <= step - 2 < CHUNKS:
            stage_three(step - 2)

    for copy in pos_copies():
        copy.wait_recv()
    for g in range(CHUNKS):
        first_copies(g)[4].wait_recv()
        for copy in second_copies(g)[4:]:
            copy.wait_recv()
        third_copies(g)[0].wait_recv()

    def column(line):
        parts = []
        for at in range(0, BLOCK, D):
            parts.append(jnp.transpose(jnp.broadcast_to(line[:, at:at + D], (D, D))))
        return jnp.concatenate(parts, axis=0)

    def dot_t(a, b):
        return lax.dot_general(a, b, (((1,), (1,)), ((), ())), preferred_element_type=jnp.float32)

    def tile(dy):
        queries = qbuf[dy]
        q_place = column(qpos[dy])[:, 0:1]
        top = jnp.full((BLOCK, D), NEG, jnp.float32)
        for b in range(KB):
            scores = dot_t(queries[:, D:], kbuf[b, :, 0:D])
            scores = jnp.where(kpos[b] <= q_place, scores, NEG)
            s_buf[:, b * BLOCK:(b + 1) * BLOCK] = scores
            top = jnp.maximum(top, jnp.maximum(scores[:, :D], scores[:, D:]))
        top = jnp.max(top, axis=1, keepdims=True)
        total = jnp.zeros((BLOCK, D), jnp.float32)
        mass = jnp.zeros((BLOCK, D), jnp.float32)
        for b in range(KB):
            cols = pl.ds(b * BLOCK, BLOCK)
            expo = jnp.exp2((s_buf[:, cols] - top) * (SCALE * LOG2E))
            weighted = expo * dot_t(queries, kbuf[b, :, 0:2 * D])
            total = total + (expo[:, :D] + expo[:, D:])
            mass = mass + (weighted[:, :D] + weighted[:, D:])
            p_buf[:, cols] = expo.astype(jnp.bfloat16)
            w_buf[:, cols] = weighted.astype(jnp.bfloat16)
        total = jnp.sum(total, axis=1, keepdims=True)
        mass = jnp.sum(mass, axis=1, keepdims=True)
        both = jnp.zeros((BLOCK, 2 * D), jnp.float32)
        third = jnp.zeros((BLOCK, D), jnp.float32)
        for b in range(KB):
            cols = pl.ds(b * BLOCK, BLOCK)
            both = both + jnp.dot(p_buf[:, cols], kbuf[b, :, 2 * D:], preferred_element_type=jnp.float32)
            third = third + jnp.dot(w_buf[:, cols], kbuf[b, :, 2 * D:3 * D], preferred_element_type=jnp.float32)
        inverse = 1.0 / total
        mean = mass * (SCALE * inverse)
        mixed = both[:, :D] * inverse
        tangent = (third * SCALE + both[:, D:]) * inverse - mean * mixed
        lanes = lax.broadcasted_iota(jnp.int32, (BLOCK, D), 1)
        stats = jnp.where(lanes == 0, top * (SCALE * LOG2E), jnp.where(lanes == 1, total, mean))
        stats = jnp.concatenate(
            [jnp.transpose(stats[at:at + D])[0:8] for at in range(0, BLOCK, D)], axis=1)
        return mixed, tangent, stats

    def o_copies(dy):
        to = along_y(dy)
        return (
            pltpu.make_async_remote_copy(
                part.at[dy], opart.at[dy], o_send.at[dy], o_recv.at[dy],
                device_id=to, device_id_type=MESH),
            pltpu.make_async_remote_copy(
                pstat.at[dy], ostat.at[dy], st_send.at[dy], st_recv.at[dy],
                device_id=to, device_id_type=MESH),
        )

    def tile_step(i, carry):
        dy = 4 - i
        mixed, tangent, stats = tile(dy)
        part[dy, :, 0:D] = mixed.astype(jnp.bfloat16)
        part[dy, :, D:] = tangent.astype(jnp.bfloat16)
        pstat[dy] = stats
        for copy in o_copies(dy):
            copy.start()
        return carry

    lax.fori_loop(1, QB, tile_step, 0)
    mixed, tangent, stats = tile(0)

    for dy in (1, 2, 3):
        for copy in o_copies(dy):
            copy.wait_recv()
    tops = [stats[0:1]] + [ostat[dy, 0:1, :] for dy in (1, 2, 3)]
    totals = [stats[1:2]] + [ostat[dy, 1:2, :] for dy in (1, 2, 3)]
    means = [stats[2:3]] + [ostat[dy, 2:3, :] for dy in (1, 2, 3)]
    top = jnp.maximum(jnp.maximum(tops[0], tops[1]), jnp.maximum(tops[2], tops[3]))
    shares = [t * jnp.exp2(m - top) for t, m in zip(totals, tops)]
    inverse = 1.0 / (shares[0] + shares[1] + shares[2] + shares[3])
    shares = [share * inverse for share in shares]
    mean = sum(share * m for share, m in zip(shares, means))
    shifts = [share * (m - mean) for share, m in zip(shares, means)]
    table = jnp.concatenate(shares + shifts + [jnp.zeros((D - 8, BLOCK), jnp.float32)], axis=0)
    table = jnp.concatenate(
        [jnp.transpose(table[:, at:at + D]) for at in range(0, BLOCK, D)], axis=0)
    mixed_all = table[:, 0:1] * mixed
    tangent_all = table[:, 0:1] * tangent + table[:, 4:5] * mixed
    for dy in (1, 2, 3):
        other = opart[dy, :, 0:D].astype(jnp.float32)
        mixed_all = mixed_all + table[:, dy:dy + 1] * other
        tangent_all = tangent_all + (
            table[:, dy:dy + 1] * opart[dy, :, D:].astype(jnp.float32)
            + table[:, 4 + dy:5 + dy] * other)
    obuf[:, 0:D] = mixed_all.astype(jnp.bfloat16)
    obuf[:, D:] = tangent_all.astype(jnp.bfloat16)

    def f_copy(i):
        slot = pl.ds(pl.multiple_of(i * ROWS, ROWS), ROWS)
        return pltpu.make_async_remote_copy(
            obuf.at[slot, :], rbuf.at[i], f_send.at[i], f_recv.at[i],
            device_id=along_z(offset(i)), device_id_type=MESH)

    def f_start(i, carry):
        f_copy(i).start()
        return carry

    lax.fori_loop(1, NZ, f_start, 0)
    rbuf[0] = obuf[0:ROWS, :]

    def drain(i, carry):
        for copy in z_copies(i):
            copy.wait_send()
        return carry

    lax.fori_loop(1, NZ, drain, 0)
    for copy in pos_copies():
        copy.wait_send()
    for g in range(CHUNKS):
        for copy in first_copies(g) + second_copies(g) + third_copies(g):
            copy.wait_send()
    for dy in (1, 2, 3):
        for copy in o_copies(dy):
            copy.wait_send()

    def finish(i, carry):
        f_copy(i).wait_recv()
        cols = pl.ds(pl.multiple_of(((z - offset(i) + NZ) % NZ) * D, D), D)
        out_ref[:, cols] = rbuf[i, :, 0:D]
        tan_ref[:, cols] = rbuf[i, :, D:]
        return carry

    cols = pl.ds(pl.multiple_of(z * D, D), D)
    out_ref[:, cols] = rbuf[0, :, 0:D]
    tan_ref[:, cols] = rbuf[0, :, D:]
    lax.fori_loop(1, NZ, finish, 0)

    def close(i, carry):
        f_copy(i).wait_send()
        return carry

    lax.fori_loop(1, NZ, close, 0)


def local(*args):
    dma = pltpu.SemaphoreType.DMA
    bf16, f32, i32 = jnp.bfloat16, jnp.float32, jnp.int32
    shape = jax.ShapeDtypeStruct((ROWS, NZ * D), bf16)
    return pl.pallas_call(
        kernel,
        out_shape=(shape, shape),
        in_specs=[pl.BlockSpec(memory_space=pltpu.VMEM)] * 6 + [pl.BlockSpec(memory_space=pltpu.SMEM)],
        out_specs=(pl.BlockSpec(memory_space=pltpu.VMEM),) * 2,
        scratch_shapes=[
            pltpu.VMEM((BLOCK, 4 * D), bf16),
            pltpu.VMEM((BLOCK, 2 * D), bf16),
            pltpu.VMEM((1, D), i32),
            pltpu.VMEM((KB, BLOCK, 4 * D), bf16),
            pltpu.VMEM((QB, BLOCK, 2 * D), bf16),
            pltpu.VMEM((NZ, 1, D), i32),
            pltpu.VMEM((KB, 1, BLOCK), i32),
            pltpu.VMEM((QB, 1, BLOCK), i32),
            pltpu.VMEM((BLOCK, KB * BLOCK), f32),
            pltpu.VMEM((BLOCK, KB * BLOCK), bf16),
            pltpu.VMEM((BLOCK, KB * BLOCK), bf16),
            pltpu.VMEM((QB, BLOCK, 2 * D), bf16),
            pltpu.VMEM((QB, 8, BLOCK), f32),
            pltpu.VMEM((QB, BLOCK, 2 * D), bf16),
            pltpu.VMEM((QB, 8, BLOCK), f32),
            pltpu.VMEM((BLOCK, 2 * D), bf16),
            pltpu.VMEM((NZ, ROWS, 2 * D), bf16),
            dma((NZ,)), dma((NZ,)), dma((NZ,)), dma((NZ,)), dma((NZ,)), dma((NZ,)),
            dma((CHUNKS * KB,)), dma((CHUNKS * KB,)), dma((CHUNKS * QB,)), dma((CHUNKS * QB,)),
            dma((KB,)), dma((KB,)), dma((QB,)), dma((QB,)),
            dma((QB,)), dma((QB,)), dma((QB,)), dma((QB,)),
            dma((NZ,)), dma((NZ,)),
        ],
        compiler_params=pltpu.CompilerParams(
            collective_id=0, has_side_effects=True, vmem_limit_bytes=40 * 2 ** 20),
    )(*args)


def solution(mesh):
    rows = P(("seq", "head"), None)
    return jax.shard_map(
        local,
        mesh=mesh,
        in_specs=(rows,) * 6 + (P(("seq", "head")),),
        out_specs=(rows, rows),
        check_vma=False,
    )
```

time: 913 us -> 82.2 us (0.09)
  the two profiles are of different devices: /device:TPU:2 before, /device:TPU:32 now
where the time goes in v1:
time: 82.2 us; the launch traced here: 81.8 us
  Pallas kernels  74.2 us (90%)
  local copies, waits for them, and re-layouts  6.94 us (8%)
    pallas_call x1, Pallas kernels, local(): pl.pallas_call(kernel, out_shape=(shape, shape), in_specs=[pl.BlockSpec(m...  74.2 us
    unnamed x16, local copies, waits for them, and re-layouts  6.94 us

profile of v1, /device:TPU:32, one launch (start us, length us, event | category | flops | bytes accessed | tf_op | source)
XLA Modules:
  0.0 81.8 jit_solution(7835918993802542079)
XLA Ops:
  0.6 0.0 copy-start
  0.6 0.8 %copy-done = bf16[16,2048]{1,0:T(8,128)(2,1)S(1)} copy-done((bf16[16,2048]{1,0:T(8,128)(2,1)S(1)}, bf16[16,2048]{1,0:T(8,128)(2,1)}, u32[]{:S(2)}) %copy-start) | copy-done | bytes 65560
  1.5 0.0 copy-start.1
  1.5 0.8 %copy-done.1 = bf16[16,2048]{1,0:T(8,128)(2,1)S(1)} copy-done((bf16[16,2048]{1,0:T(8,128)(2,1)S(1)}, bf16[16,2048]{1,0:T(8,128)(2,1)}, u32[]{:S(2)}) %copy-start.1) | copy-done | bytes 65560
  2.3 0.0 copy-start.2
  2.3 0.8 %copy-done.2 = bf16[16,2048]{1,0:T(8,128)(2,1)S(1)} copy-done((bf16[16,2048]{1,0:T(8,128)(2,1)S(1)}, bf16[16,2048]{1,0:T(8,128)(2,1)}, u32[]{:S(2)}) %copy-start.2) | copy-done | bytes 65560
  3.2 0.0 copy-start.3
  3.2 0.8 %copy-done.3 = bf16[16,2048]{1,0:T(8,128)(2,1)S(1)} copy-done((bf16[16,2048]{1,0:T(8,128)(2,1)S(1)}, bf16[16,2048]{1,0:T(8,128)(2,1)}, u32[]{:S(2)}) %copy-start.3) | copy-done | bytes 65560
  4.0 0.0 copy-start.4
  4.0 0.8 %copy-done.4 = bf16[16,2048]{1,0:T(8,128)(2,1)S(1)} copy-done((bf16[16,2048]{1,0:T(8,128)(2,1)S(1)}, bf16[16,2048]{1,0:T(8,128)(2,1)}, u32[]{:S(2)}) %copy-start.4) | copy-done | bytes 65560
  4.8 0.0 copy-start.5
  4.8 0.8 %copy-done.5 = bf16[16,2048]{1,0:T(8,128)(2,1)S(1)} copy-done((bf16[16,2048]{1,0:T(8,128)(2,1)S(1)}, bf16[16,2048]{1,0:T(8,128)(2,1)}, u32[]{:S(2)}) %copy-start.5) | copy-done | bytes 65560
  5.7 0.0 copy-start.6
  5.7 0.7 copy-done.6
  6.3 74.2 %shard_map.86 = (bf16[16,2048]{1,0:T(8,128)(2,1)S(1)}, bf16[16,2048]{1,0:T(8,128)(2,1)S(1)}) custom-call(bf16[16,2048]{1,0:T(8,128)(2,1)S(1)} %copy-done, bf16[16,2048]{1,0:T(8,128)(2,1)S(1)} %copy-done.1, bf16[16,2048]{1,0:T(8,128)(2,1)S(1)} %copy-done.2, bf16[16,2048]{1,0:T(8,128)(2,1)S(1)} %copy-done.3, bf16[16,2048]{1,0:T(8,128)(2,1)S(1)} %copy-done.4, ...), custom_call_target="tpu_custom_call" | custom-call | tf_op jit(solution)/shard_map/pallas_call | solution.py:366
  80.5 0.6 copy.11
  81.1 0.6 copy.12
Async XLA Ops:
  0.6 0.8 %copy-start = (bf16[16,2048]{1,0:T(8,128)(2,1)S(1)}, bf16[16,2048]{1,0:T(8,128)(2,1)}, u32[]{:S(2)}) copy-start(bf16[16,2048]{1,0:T(8,128)(2,1)} %q_ref.1) | copy-start | bytes 196612
  1.5 0.8 %copy-start.1 = (bf16[16,2048]{1,0:T(8,128)(2,1)S(1)}, bf16[16,2048]{1,0:T(8,128)(2,1)}, u32[]{:S(2)}) copy-start(bf16[16,2048]{1,0:T(8,128)(2,1)} %k_ref.1) | copy-start | bytes 196612
  2.3 0.8 %copy-start.2 = (bf16[16,2048]{1,0:T(8,128)(2,1)S(1)}, bf16[16,2048]{1,0:T(8,128)(2,1)}, u32[]{:S(2)}) copy-start(bf16[16,2048]{1,0:T(8,128)(2,1)} %v_ref.1) | copy-start | bytes 196612
  3.2 0.8 %copy-start.3 = (bf16[16,2048]{1,0:T(8,128)(2,1)S(1)}, bf16[16,2048]{1,0:T(8,128)(2,1)}, u32[]{:S(2)}) copy-start(bf16[16,2048]{1,0:T(8,128)(2,1)} %dq_ref.1) | copy-start | bytes 196612
  4.0 0.8 %copy-start.4 = (bf16[16,2048]{1,0:T(8,128)(2,1)S(1)}, bf16[16,2048]{1,0:T(8,128)(2,1)}, u32[]{:S(2)}) copy-start(bf16[16,2048]{1,0:T(8,128)(2,1)} %dk_ref.1) | copy-start | bytes 196612
  4.8 0.8 %copy-start.5 = (bf16[16,2048]{1,0:T(8,128)(2,1)S(1)}, bf16[16,2048]{1,0:T(8,128)(2,1)}, u32[]{:S(2)}) copy-start(bf16[16,2048]{1,0:T(8,128)(2,1)} %dv_ref.1) | copy-start | bytes 196612
  5.7 0.7 copy-start.6

commit v2 on v0

v2 whole, which is shorter than its diff:
```python
import jax
import jax.numpy as jnp
from jax import lax
from jax.experimental import pallas as pl
from jax.experimental.pallas import tpu as pltpu
from jax.sharding import PartitionSpec as P

D = 128
NZ = 16
ROWS = 16
BLOCK = NZ * ROWS
HALF = BLOCK // 2
KB = 8
QB = 4
SCALE = D ** -0.5
LOG2E = 1.4426950408889634
NEG = -1e30
MESH = pl.DeviceIdType.MESH
DISTANCES = (2, 1, 3, 0)
OWN = NZ - 1


def offset(slot):
    i = NZ - 1 - slot
    return ((i + 1) // 2) * (2 * (i % 2) - 1)


def loop(start, stop, body):
    def step(i, carry):
        body(i)
        return carry

    lax.fori_loop(start, stop, step, 0)


def dot_t(a, b):
    return lax.dot_general(a, b, (((1,), (1,)), ((), ())), preferred_element_type=jnp.float32)


def kernel(q_hbm, k_hbm, v_hbm, dq_hbm, dk_hbm, dv_hbm, pos_hbm,
           out_ref, tan_ref,
           q_ref, k_ref, v_ref, dq_ref, dk_ref, dv_ref, pos_ref, in_sem,
           kpack, vpack, qpack, prow, kbuf, vbuf, qbuf, pbuf, kpos, qpos,
           s_buf, p_buf, w_buf, part, pstat, opart, ostat, obuf, rbuf,
           zk_send, zk_recv, zv_send, zv_recv, zq_send, zq_recv, zp_send, zp_recv,
           k_send, k_recv, v_send, v_recv, q_send, q_recv,
           kp_send, kp_recv, qp_send, qp_recv,
           o_send, o_recv, st_send, st_recv, f_send, f_recv):
    s = lax.axis_index("seq")
    h = lax.axis_index("head")
    c = s % 2
    z = (s // 2) % NZ
    y = (h % 2) * 2 + s // (2 * NZ)
    x = h // 2

    def device(x_, y_, z_, c_):
        return (((y_ % 2) * NZ + z_) * 2 + c_, x_ * 2 + y_ // 2)

    def along_z(by):
        return device(x, y, (z + by + NZ) % NZ, c)

    def along_x(by):
        return device((x + by) % 4, y, z, c)

    def across_x(by):
        return device((x + by) % 4, y, z, 1 - c)

    def along_y(by):
        return device(x, (y + by) % 4, z, c)

    twin = device(x, y, z, 1 - c)

    def send(source, target, send_sem, recv_sem, to):
        return pltpu.make_async_remote_copy(
            source, target, send_sem, recv_sem, device_id=to, device_id_type=MESH)

    fetches = [
        pltpu.make_async_copy(source, held, in_sem.at[i])
        for i, (source, held) in enumerate((
            (k_hbm, k_ref), (dk_hbm, dk_ref), (pos_hbm, pos_ref), (v_hbm, v_ref), (dv_hbm, dv_ref),
            (dq_hbm, dq_ref), (q_hbm, q_ref)))
    ]
    for fetch in fetches:
        fetch.start()

    barrier = pltpu.get_barrier_semaphore()

    def greet(to):
        pl.semaphore_signal(barrier, inc=1, device_id=to, device_id_type=MESH)

    loop(1, NZ, lambda i: greet(along_z(i)))
    for by in (1, 2, 3):
        greet(along_x(by))
        greet(across_x(by))
        greet(along_y(by))
    greet(twin)

    own = pl.ds(pl.multiple_of(z * ROWS, ROWS), ROWS)

    def pack(left, right, packed, place):
        for head in range(NZ):
            rows = pl.ds(head * ROWS, ROWS)
            cols = pl.ds(head * D, D)
            packed[rows, 0:D] = left[:, cols]
            packed[rows, D:] = right[:, cols]
        place[...] = packed[own, :]

    for fetch in fetches[:3]:
        fetch.wait()
    pack(k_ref, dk_ref, kpack, kbuf.at[0, OWN * ROWS:, :])
    lane = lax.broadcasted_iota(jnp.int32, (1, D), 1)
    row = jnp.zeros((1, D), jnp.int32)
    for i in range(ROWS):
        row = jnp.where(lane % ROWS == i, pos_ref[i], row)
    prow[...] = row
    pbuf[OWN] = row

    pl.semaphore_wait(barrier, NZ - 1 + 10)

    def z_copy(packed, buf, send_sem, recv_sem, i):
        by = offset(i)
        source = pl.ds(pl.multiple_of(((z - by + NZ) % NZ) * ROWS, ROWS), ROWS)
        slot = pl.ds(pl.multiple_of(i * ROWS, ROWS), ROWS)
        if buf is qbuf:
            slot = pl.ds(pl.multiple_of(3 * HALF + (i % 8) * ROWS, ROWS), ROWS)
            target = buf.at[i // 8, slot, :]
        else:
            target = buf.at[0, slot, :]
        return send(packed.at[source, :], target, send_sem.at[i], recv_sem.at[i], along_z(-by))

    def zk(i):
        return z_copy(kpack, kbuf, zk_send, zk_recv, i)

    def zv(i):
        return z_copy(vpack, vbuf, zv_send, zv_recv, i)

    def zq(i):
        return z_copy(qpack, qbuf, zq_send, zq_recv, i)

    def zp(i):
        return send(prow, pbuf.at[i], zp_send.at[i], zp_recv.at[i], along_z(-offset(i)))

    def gather(buf, send_sem, recv_sem):
        def copy(block, rows, to, at, sem):
            return send(buf.at[block, rows, :], buf.at[at, rows, :], send_sem.at[sem], recv_sem.at[sem], to)

        every = pl.ds(0, BLOCK)
        first = lambda: [
            copy(0, every, along_x(2), 4, 4),
            copy(0, every, along_x(1), 6, 6),
            copy(0, every, along_x(3), 2, 2),
            copy(0, every, twin, 1, 1),
        ]
        second = lambda: [copy(block, every, twin, block + 1, block + 1) for block in (2, 6, 4)]
        return first, second

    k_first, k_second = gather(kbuf, k_send, k_recv)
    v_first, v_second = gather(vbuf, v_send, v_recv)

    def group(dy):
        return pl.ds(DISTANCES.index(dy) * HALF, HALF)

    def q_copy(half, dy):
        sem = half * 4 + dy
        return send(qbuf.at[half, group(0), :], qbuf.at[half, group(dy), :],
                    q_send.at[sem], q_recv.at[sem], along_y(4 - dy))

    def q_copies(half):
        return [q_copy(half, dy) for dy in (2, 1, 3)]

    def kp_copy(to, at):
        return send(kpos.at[0], kpos.at[at], kp_send.at[at], kp_recv.at[at], to)

    def qp_copy(to, at):
        return send(kpos.at[0], qpos.at[at], qp_send.at[at], qp_recv.at[at], to)

    def pos_copies():
        copies = [kp_copy(twin, 1)]
        for by in (1, 2, 3):
            copies.append(kp_copy(along_x(4 - by), 2 * by))
            copies.append(kp_copy(across_x(4 - by), 2 * by + 1))
            copies.append(qp_copy(along_y(4 - by), by))
        return copies

    def start_all(copies):
        for copy in copies:
            copy.start()

    def wait_recv_all(copies):
        for copy in copies:
            copy.wait_recv()

    def first_z(i):
        zk(i).start()
        zp(i).start()

    loop(0, OWN, first_z)
    for fetch in fetches[3:5]:
        fetch.wait()
    pack(v_ref, dv_ref, vpack, vbuf.at[0, OWN * ROWS:, :])

    def values_z(i):
        zk(i).wait_send()
        zv(i).start()

    def queries_z(i):
        zv(i).wait_send()
        zq(i).start()

    loop(0, OWN, values_z)
    for fetch in fetches[5:]:
        fetch.wait()
    pack(dq_ref, q_ref, qpack, qbuf.at[1, 4 * HALF - ROWS:, :])
    loop(0, OWN, lambda i: zk(i).wait_recv())
    start_all(k_first())
    loop(0, OWN, lambda i: zp(i).wait_recv())
    total = []
    for g in range(2):
        line = jnp.zeros((1, D), jnp.int32)
        for i in range(8):
            line = jnp.where(lane // ROWS == i, pbuf[g * 8 + i], line)
        total.append(line)
    line = jnp.concatenate(total, axis=1)
    kpos[0] = line
    qpos[0] = line
    start_all(pos_copies())
    loop(0, OWN, queries_z)
    wait_recv_all(k_first()[:3])
    start_all(k_second())
    loop(0, OWN, lambda i: zv(i).wait_recv())
    start_all(v_first())
    loop(0, NZ // 2, lambda i: zq(i).wait_recv())
    start_all(q_copies(0))
    loop(NZ // 2, OWN, lambda i: zq(i).wait_recv())
    start_all(q_copies(1))
    wait_recv_all(v_first()[:3])
    start_all(v_second())
    wait_recv_all(pos_copies())
    wait_recv_all(k_first()[3:] + k_second())
    wait_recv_all(v_first()[3:] + v_second())

    def tile(half, pair):
        rows = pl.ds(pl.multiple_of(pair * BLOCK, BLOCK), BLOCK)
        queries = qbuf[half, rows, :]
        dys = (DISTANCES[0] + pair * (DISTANCES[2] - DISTANCES[0]), DISTANCES[1] + pair * (DISTANCES[3] - DISTANCES[1]))
        places = []
        for dy in dys:
            line = qpos[dy, :, pl.ds(pl.multiple_of(half * HALF, HALF), HALF)]
            places.append(jnp.transpose(jnp.broadcast_to(line, (HALF, HALF))))
        places = jnp.concatenate(places, axis=0)[:, 0:1]
        top = jnp.full((BLOCK, D), NEG, jnp.float32)
        for b in range(KB):
            scores = dot_t(queries[:, D:], kbuf[b, :, 0:D])
            scores = jnp.where(kpos[b] <= places, scores, NEG)
            s_buf[:, b * BLOCK:(b + 1) * BLOCK] = scores
            top = jnp.maximum(top, jnp.maximum(scores[:, :D], scores[:, D:]))
        top = jnp.max(top, axis=1, keepdims=True)
        total = jnp.zeros((BLOCK, D), jnp.float32)
        mass = jnp.zeros((BLOCK, D), jnp.float32)
        for b in range(KB):
            cols = pl.ds(b * BLOCK, BLOCK)
            expo = jnp.exp2((s_buf[:, cols] - top) * (SCALE * LOG2E))
            weighted = expo * dot_t(queries, kbuf[b])
            total = total + (expo[:, :D] + expo[:, D:])
            mass = mass + (weighted[:, :D] + weighted[:, D:])
            p_buf[:, cols] = expo.astype(jnp.bfloat16)
            w_buf[:, cols] = weighted.astype(jnp.bfloat16)
        total = jnp.sum(total, axis=1, keepdims=True)
        mass = jnp.sum(mass, axis=1, keepdims=True)
        both = jnp.zeros((BLOCK, 2 * D), jnp.float32)
        third = jnp.zeros((BLOCK, D), jnp.float32)
        for b in range(KB):
            cols = pl.ds(b * BLOCK, BLOCK)
            both = both + jnp.dot(p_buf[:, cols], vbuf[b], preferred_element_type=jnp.float32)
            third = third + jnp.dot(w_buf[:, cols], vbuf[b, :, 0:D], preferred_element_type=jnp.float32)
        inverse = 1.0 / total
        mean = mass * (SCALE * inverse)
        mixed = both[:, :D] * inverse
        tangent = (third * SCALE + both[:, D:]) * inverse - mean * mixed
        lanes = lax.broadcasted_iota(jnp.int32, (BLOCK, D), 1)
        stats = jnp.where(lanes == 0, top * (SCALE * LOG2E), jnp.where(lanes == 1, total, mean))
        part[half, rows, 0:D] = mixed.astype(jnp.bfloat16)
        part[half, rows, D:] = tangent.astype(jnp.bfloat16)
        for at, dy in enumerate(dys):
            pstat[half * 4 + dy] = jnp.transpose(stats[at * HALF:(at + 1) * HALF])[0:8]

    def o_copy(half, dy):
        sem = half * 4 + dy
        return send(part.at[half, group(dy), :], opart.at[half, group(dy), :],
                    o_send.at[sem], o_recv.at[sem], along_y(dy))

    def st_copy(half, dy):
        sem = half * 4 + dy
        return send(pstat.at[sem], ostat.at[sem], st_send.at[sem], st_recv.at[sem], along_y(dy))

    def f_copy(i):
        slot = pl.ds(pl.multiple_of(i * ROWS, ROWS), ROWS)
        return send(obuf.at[slot, :], rbuf.at[i], f_send.at[i], f_recv.at[i], along_z(offset(i)))

    def merge(half):
        for dy in (1, 2, 3):
            o_copy(half, dy).wait_recv()
            st_copy(half, dy).wait_recv()
        rows = pl.ds(half * HALF, HALF)
        lines = [pstat[half * 4]] + [ostat[half * 4 + dy] for dy in (1, 2, 3)]
        tops = [line[0:1] for line in lines]
        top = jnp.maximum(jnp.maximum(tops[0], tops[1]), jnp.maximum(tops[2], tops[3]))
        shares = [line[1:2] * jnp.exp2(line[0:1] - top) for line in lines]
        inverse = 1.0 / (shares[0] + shares[1] + shares[2] + shares[3])
        shares = [share * inverse for share in shares]
        mean = sum(share * line[2:3] for share, line in zip(shares, lines))
        shifts = [share * (line[2:3] - mean) for share, line in zip(shares, lines)]
        table = jnp.concatenate(shares + shifts + [jnp.zeros((D - 8, HALF), jnp.float32)], axis=0)
        table = jnp.transpose(table)
        mixed = jnp.zeros((HALF, D), jnp.float32)
        tangent = jnp.zeros((HALF, D), jnp.float32)
        for dy in range(QB):
            held = part if dy == 0 else opart
            one = held[half, group(dy), 0:D].astype(jnp.float32)
            two = held[half, group(dy), D:].astype(jnp.float32)
            mixed = mixed + table[:, dy:dy + 1] * one
            tangent = tangent + (table[:, dy:dy + 1] * two + table[:, 4 + dy:5 + dy] * one)
        obuf[rows, 0:D] = mixed.astype(jnp.bfloat16)
        obuf[rows, D:] = tangent.astype(jnp.bfloat16)
        loop(half * NZ // 2, min(OWN, (half + 1) * NZ // 2), lambda i: f_copy(i).start())

    def o_start(half, dy):
        o_copy(half, dy).start()
        st_copy(half, dy).start()

    def tile_step(i):
        half = i // 2
        pair = i % 2

        @pl.when(pair == 0)
        def _():
            q_copy(half, 2).wait_recv()
            q_copy(half, 1).wait_recv()

        @pl.when(pair == 1)
        def _():
            q_copy(half, 3).wait_recv()

        tile(half, pair)

        @pl.when(pair == 0)
        def _():
            o_start(half, 2)
            o_start(half, 1)

        @pl.when(pair == 1)
        def _():
            o_start(half, 3)

    loop(0, 4, tile_step)
    merge(0)
    merge(1)

    def drain(i):
        for copy in (zp(i), zq(i)):
            copy.wait_send()

    loop(0, OWN, drain)
    sent = pos_copies() + k_first() + k_second() + v_first() + v_second()
    for half in range(2):
        sent += q_copies(half)
        for dy in (1, 2, 3):
            sent += [o_copy(half, dy), st_copy(half, dy)]
    for copy in sent:
        copy.wait_send()

    def place(head, held):
        cols = pl.ds(pl.multiple_of(head * D, D), D)
        out_ref[:, cols] = held[:, 0:D]
        tan_ref[:, cols] = held[:, D:]

    place(z, obuf[OWN * ROWS:, :])

    def finish(i):
        f_copy(i).wait_recv()
        place((z - offset(i) + NZ) % NZ, rbuf[i])

    loop(0, OWN, finish)
    loop(0, OWN, lambda i: f_copy(i).wait_send())


def local(*args):
    dma = pltpu.SemaphoreType.DMA
    bf16, f32, i32 = jnp.bfloat16, jnp.float32, jnp.int32
    shape = jax.ShapeDtypeStruct((ROWS, NZ * D), bf16)
    return pl.pallas_call(
        kernel,
        out_shape=(shape, shape),
        in_specs=[pl.BlockSpec(memory_space=pl.ANY)] * 7,
        out_specs=(pl.BlockSpec(memory_space=pltpu.VMEM),) * 2,
        scratch_shapes=[pltpu.VMEM((ROWS, NZ * D), bf16)] * 6 + [
            pltpu.SMEM((ROWS,), i32),
            dma((7,)),
            pltpu.VMEM((BLOCK, 2 * D), bf16),
            pltpu.VMEM((BLOCK, 2 * D), bf16),
            pltpu.VMEM((BLOCK, 2 * D), bf16),
            pltpu.VMEM((1, D), i32),
            pltpu.VMEM((KB, BLOCK, 2 * D), bf16),
            pltpu.VMEM((KB, BLOCK, 2 * D), bf16),
            pltpu.VMEM((2, QB * HALF, 2 * D), bf16),
            pltpu.VMEM((NZ, 1, D), i32),
            pltpu.VMEM((KB, 1, BLOCK), i32),
            pltpu.VMEM((QB, 1, BLOCK), i32),
            pltpu.VMEM((BLOCK, KB * BLOCK), f32),
            pltpu.VMEM((BLOCK, KB * BLOCK), bf16),
            pltpu.VMEM((BLOCK, KB * BLOCK), bf16),
            pltpu.VMEM((2, QB * HALF, 2 * D), bf16),
            pltpu.VMEM((2 * QB, 8, HALF), f32),
            pltpu.VMEM((2, QB * HALF, 2 * D), bf16),
            pltpu.VMEM((2 * QB, 8, HALF), f32),
            pltpu.VMEM((BLOCK, 2 * D), bf16),
            pltpu.VMEM((NZ, ROWS, 2 * D), bf16),
        ] + [dma((NZ,))] * 8 + [dma((KB,))] * 4 + [dma((2 * QB,))] * 2
        + [dma((KB,))] * 2 + [dma((QB,))] * 2 + [dma((2 * QB,))] * 4 + [dma((NZ,))] * 2,
        compiler_params=pltpu.CompilerParams(
            collective_id=0, has_side_effects=True, vmem_limit_bytes=40 * 2 ** 20),
    )(*args)


def solution(mesh):
    rows = P(("seq", "head"), None)
    return jax.shard_map(
        local,
        mesh=mesh,
        in_specs=(rows,) * 6 + (P(("seq", "head")),),
        out_specs=(rows, rows),
        check_vma=False,
    )
```

time: 913 us -> 69.8 us (0.08)
  the two profiles are of different devices: /device:TPU:2 before, /device:TPU:9 now
where the time goes in v2:
time: 69.8 us; the launch traced here: 69.4 us
  Pallas kernels  61.8 us (89%)
  local copies, waits for them, and re-layouts  6.94 us (10%)
    pallas_call x1, Pallas kernels, local(): pl.pallas_call(kernel, out_shape=(shape, shape), in_specs=[pl.BlockSpec(m...  61.8 us
    unnamed x16, local copies, waits for them, and re-layouts  6.94 us

profile of v2, /device:TPU:9, one launch (start us, length us, event | category | flops | bytes accessed | tf_op | source)
XLA Modules:
  0.0 69.4 jit_solution(12723272203360505841)
XLA Ops:
  0.6 0.0 copy-start
  0.6 0.8 %copy-done = bf16[16,2048]{1,0:T(8,128)(2,1)S(1)} copy-done((bf16[16,2048]{1,0:T(8,128)(2,1)S(1)}, bf16[16,2048]{1,0:T(8,128)(2,1)}, u32[]{:S(2)}) %copy-start) | copy-done | bytes 65560
  1.5 0.0 copy-start.1
  1.5 0.8 %copy-done.1 = bf16[16,2048]{1,0:T(8,128)(2,1)S(1)} copy-done((bf16[16,2048]{1,0:T(8,128)(2,1)S(1)}, bf16[16,2048]{1,0:T(8,128)(2,1)}, u32[]{:S(2)}) %copy-start.1) | copy-done | bytes 65560
  2.3 0.0 copy-start.2
  2.3 0.8 %copy-done.2 = bf16[16,2048]{1,0:T(8,128)(2,1)S(1)} copy-done((bf16[16,2048]{1,0:T(8,128)(2,1)S(1)}, bf16[16,2048]{1,0:T(8,128)(2,1)}, u32[]{:S(2)}) %copy-start.2) | copy-done | bytes 65560
  3.2 0.0 copy-start.3
  3.2 0.8 %copy-done.3 = bf16[16,2048]{1,0:T(8,128)(2,1)S(1)} copy-done((bf16[16,2048]{1,0:T(8,128)(2,1)S(1)}, bf16[16,2048]{1,0:T(8,128)(2,1)}, u32[]{:S(2)}) %copy-start.3) | copy-done | bytes 65560
  4.0 0.0 copy-start.4
  4.0 0.8 %copy-done.4 = bf16[16,2048]{1,0:T(8,128)(2,1)S(1)} copy-done((bf16[16,2048]{1,0:T(8,128)(2,1)S(1)}, bf16[16,2048]{1,0:T(8,128)(2,1)}, u32[]{:S(2)}) %copy-start.4) | copy-done | bytes 65560
  4.8 0.0 copy-start.5
  4.8 0.8 %copy-done.5 = bf16[16,2048]{1,0:T(8,128)(2,1)S(1)} copy-done((bf16[16,2048]{1,0:T(8,128)(2,1)S(1)}, bf16[16,2048]{1,0:T(8,128)(2,1)}, u32[]{:S(2)}) %copy-start.5) | copy-done | bytes 65560
  5.7 0.0 copy-start.6
  5.7 0.7 copy-done.6
  6.3 61.8 %shard_map.86 = (bf16[16,2048]{1,0:T(8,128)(2,1)S(1)}, bf16[16,2048]{1,0:T(8,128)(2,1)S(1)}) custom-call(bf16[16,2048]{1,0:T(8,128)(2,1)S(1)} %copy-done, bf16[16,2048]{1,0:T(8,128)(2,1)S(1)} %copy-done.1, bf16[16,2048]{1,0:T(8,128)(2,1)S(1)} %copy-done.2, bf16[16,2048]{1,0:T(8,128)(2,1)S(1)} %copy-done.3, bf16[16,2048]{1,0:T(8,128)(2,1)S(1)} %copy-done.4, ...), custom_call_target="tpu_custom_call" | custom-call | tf_op jit(solution)/shard_map/pallas_call | solution.py:391
  68.1 0.6 copy.11
  68.8 0.6 copy.12
Async XLA Ops:
  0.6 0.8 %copy-start = (bf16[16,2048]{1,0:T(8,128)(2,1)S(1)}, bf16[16,2048]{1,0:T(8,128)(2,1)}, u32[]{:S(2)}) copy-start(bf16[16,2048]{1,0:T(8,128)(2,1)} %q_hbm.1) | copy-start | bytes 196612
  1.5 0.8 %copy-start.1 = (bf16[16,2048]{1,0:T(8,128)(2,1)S(1)}, bf16[16,2048]{1,0:T(8,128)(2,1)}, u32[]{:S(2)}) copy-start(bf16[16,2048]{1,0:T(8,128)(2,1)} %k_hbm.1) | copy-start | bytes 196612
  2.3 0.8 %copy-start.2 = (bf16[16,2048]{1,0:T(8,128)(2,1)S(1)}, bf16[16,2048]{1,0:T(8,128)(2,1)}, u32[]{:S(2)}) copy-start(bf16[16,2048]{1,0:T(8,128)(2,1)} %v_hbm.1) | copy-start | bytes 196612
  3.2 0.8 %copy-start.3 = (bf16[16,2048]{1,0:T(8,128)(2,1)S(1)}, bf16[16,2048]{1,0:T(8,128)(2,1)}, u32[]{:S(2)}) copy-start(bf16[16,2048]{1,0:T(8,128)(2,1)} %dq_hbm.1) | copy-start | bytes 196612
  4.0 0.8 %copy-start.4 = (bf16[16,2048]{1,0:T(8,128)(2,1)S(1)}, bf16[16,2048]{1,0:T(8,128)(2,1)}, u32[]{:S(2)}) copy-start(bf16[16,2048]{1,0:T(8,128)(2,1)} %dk_hbm.1) | copy-start | bytes 196612
  4.8 0.8 %copy-start.5 = (bf16[16,2048]{1,0:T(8,128)(2,1)S(1)}, bf16[16,2048]{1,0:T(8,128)(2,1)}, u32[]{:S(2)}) copy-start(bf16[16,2048]{1,0:T(8,128)(2,1)} %dv_hbm.1) | copy-start | bytes 196612
  5.7 0.7 copy-start.6

commit v3 on v2

v3 whole, which is shorter than its diff:
```python
import jax
import jax.numpy as jnp
from jax import lax
from jax.experimental import pallas as pl
from jax.experimental.pallas import tpu as pltpu
from jax.sharding import PartitionSpec as P

D = 128
NZ = 16
ROWS = 16
BLOCK = NZ * ROWS
HALF = BLOCK // 2
PART = BLOCK // 4
SLOTS = NZ // 4
KB = 8
QB = 4
SCALE = D ** -0.5
LOG2E = 1.4426950408889634
NEG = -1e30
MESH = pl.DeviceIdType.MESH
DISTANCES = (2, 1, 3, 0)
OWN = NZ - 1


def offset(slot):
    i = NZ - 1 - slot
    return ((i + 1) // 2) * (2 * (i % 2) - 1)


def loop(start, stop, body):
    def step(i, carry):
        body(i)
        return carry

    lax.fori_loop(start, stop, step, 0)


def dot_t(a, b):
    return lax.dot_general(a, b, (((1,), (1,)), ((), ())), preferred_element_type=jnp.float32)


def kernel(q_hbm, k_hbm, v_hbm, dq_hbm, dk_hbm, dv_hbm, pos_hbm,
           out_ref, tan_ref,
           q_ref, k_ref, v_ref, dq_ref, dk_ref, dv_ref, pos_ref, in_sem,
           kpack, vpack, qpack, prow, kbuf, vbuf, qbuf, pbuf, kpos, qpos, qcol,
           s_buf, p_buf, w_buf, part, pstat, opart, ostat, obuf, rbuf,
           zk_send, zk_recv, zv_send, zv_recv, zq_send, zq_recv, zp_send, zp_recv,
           k_send, k_recv, v_send, v_recv, q_send, q_recv,
           kp_send, kp_recv, qp_send, qp_recv,
           o_send, o_recv, st_send, st_recv, f_send, f_recv):
    s = lax.axis_index("seq")
    h = lax.axis_index("head")
    c = s % 2
    z = (s // 2) % NZ
    y = (h % 2) * 2 + s // (2 * NZ)
    x = h // 2

    def device(x_, y_, z_, c_):
        return (((y_ % 2) * NZ + z_) * 2 + c_, x_ * 2 + y_ // 2)

    def along_z(by):
        return device(x, y, (z + by + NZ) % NZ, c)

    def along_x(by):
        return device((x + by) % 4, y, z, c)

    def across_x(by):
        return device((x + by) % 4, y, z, 1 - c)

    def along_y(by):
        return device(x, (y + by) % 4, z, c)

    twin = device(x, y, z, 1 - c)

    def send(source, target, send_sem, recv_sem, to):
        return pltpu.make_async_remote_copy(
            source, target, send_sem, recv_sem, device_id=to, device_id_type=MESH)

    fetches = [
        pltpu.make_async_copy(source, held, in_sem.at[i])
        for i, (source, held) in enumerate((
            (k_hbm, k_ref), (dk_hbm, dk_ref), (pos_hbm, pos_ref), (v_hbm, v_ref), (dv_hbm, dv_ref),
            (dq_hbm, dq_ref), (q_hbm, q_ref)))
    ]
    for fetch in fetches:
        fetch.start()

    barrier = pltpu.get_barrier_semaphore()

    def greet(to):
        pl.semaphore_signal(barrier, inc=1, device_id=to, device_id_type=MESH)

    loop(1, NZ, lambda i: greet(along_z(i)))
    for by in (1, 2, 3):
        greet(along_x(by))
        greet(across_x(by))
        greet(along_y(by))
    greet(twin)

    own = pl.ds(pl.multiple_of(z * ROWS, ROWS), ROWS)

    def pack(left, right, packed, place):
        for head in range(NZ):
            rows = pl.ds(head * ROWS, ROWS)
            cols = pl.ds(head * D, D)
            packed[rows, 0:D] = left[:, cols]
            packed[rows, D:] = right[:, cols]
        place[...] = packed[own, :]

    for fetch in fetches[:3]:
        fetch.wait()
    pack(k_ref, dk_ref, kpack, kbuf.at[0, OWN * ROWS:, :])
    lane = lax.broadcasted_iota(jnp.int32, (1, D), 1)
    row = jnp.zeros((1, D), jnp.int32)
    for i in range(ROWS):
        row = jnp.where(lane % ROWS == i, pos_ref[i], row)
    prow[...] = row
    pbuf[OWN] = row

    pl.semaphore_wait(barrier, NZ - 1 + 10)

    def arrived(ref, sem):
        pltpu.make_async_copy(ref, ref, sem).wait()

    def z_copy(packed, buf, send_sem, recv_sem, i):
        by = offset(i)
        source = pl.ds(pl.multiple_of(((z - by + NZ) % NZ) * ROWS, ROWS), ROWS)
        slot = pl.ds(pl.multiple_of(i * ROWS, ROWS), ROWS)
        if buf is qbuf:
            slot = pl.ds(pl.multiple_of(3 * PART + (i % SLOTS) * ROWS, ROWS), ROWS)
            target = buf.at[i // SLOTS, slot, :]
        else:
            target = buf.at[0, slot, :]
        shared = i // SLOTS if buf is qbuf else i // (NZ // 2)
        return send(packed.at[source, :], target, send_sem.at[i], recv_sem.at[shared], along_z(-by))

    def zk(i):
        return z_copy(kpack, kbuf, zk_send, zk_recv, i)

    def zv(i):
        return z_copy(vpack, vbuf, zv_send, zv_recv, i)

    def zq(i):
        return z_copy(qpack, qbuf, zq_send, zq_recv, i)

    def zp(i):
        return send(prow, pbuf.at[i], zp_send, zp_recv, along_z(-offset(i)))

    def gather(buf, send_sem, recv_sem):
        def copy(block, rows, to, at, sem):
            return send(buf.at[block, rows, :], buf.at[at, rows, :], send_sem, recv_sem.at[sem], to)

        def first(half):
            rows = pl.ds(half * HALF, HALF)
            return [
                copy(0, rows, along_x(2), 4, half),
                copy(0, rows, along_x(1), 6, half),
                copy(0, rows, along_x(3), 2, half),
                copy(0, rows, twin, 1, 2),
            ]

        def first_arrived(half):
            arrived(buf.at[0:3, half * HALF:(half + 1) * HALF, :], recv_sem.at[half])

        def second(half):
            rows = pl.ds(half * HALF, HALF)
            return [copy(block, rows, twin, block + 1, 2) for block in (2, 6, 4)]

        def second_arrived():
            arrived(buf.at[0:4], recv_sem.at[2])

        def left():
            arrived(buf.at[0:7], send_sem)

        return first, first_arrived, second, second_arrived, left

    k_first, k_first_arrived, k_second, k_second_arrived, k_left = gather(kbuf, k_send, k_recv)
    v_first, v_first_arrived, v_second, v_second_arrived, v_left = gather(vbuf, v_send, v_recv)

    def group(dy):
        return pl.ds(DISTANCES.index(dy) * PART, PART)

    def q_copy(quarter, dy):
        return send(qbuf.at[quarter, group(0), :], qbuf.at[quarter, group(dy), :],
                    q_send, q_recv.at[quarter], along_y(4 - dy))

    def q_copies(quarter):
        return [q_copy(quarter, dy) for dy in (2, 1, 3)]

    def kp_copy(to, at):
        return send(kpos.at[0], kpos.at[at], kp_send, kp_recv, to)

    def qp_copy(to, at):
        return send(kpos.at[0], qpos.at[at], qp_send, qp_recv, to)

    def pos_copies():
        copies = [kp_copy(twin, 1)]
        for by in (1, 2, 3):
            copies.append(kp_copy(along_x(4 - by), 2 * by))
            copies.append(kp_copy(across_x(4 - by), 2 * by + 1))
            copies.append(qp_copy(along_y(4 - by), by))
        return copies

    def start_all(copies):
        for copy in copies:
            copy.start()

    def first_z(i):
        zk(i).start()
        zp(i).start()

    loop(0, OWN, first_z)
    for fetch in fetches[3:5]:
        fetch.wait()
    pack(v_ref, dv_ref, vpack, vbuf.at[0, OWN * ROWS:, :])

    def values_z(i):
        zk(i).wait_send()
        zv(i).start()

    def queries_z(i):
        zv(i).wait_send()
        zq(i).start()

    loop(0, OWN, values_z)
    for fetch in fetches[5:]:
        fetch.wait()
    pack(dq_ref, q_ref, qpack, qbuf.at[3, BLOCK - ROWS:, :])
    arrived(kbuf.at[0, 0:HALF, :], zk_recv.at[0])
    start_all(k_first(0))
    arrived(pbuf.at[0:OWN], zp_recv)
    total = []
    for g in range(2):
        line = jnp.zeros((1, D), jnp.int32)
        for i in range(8):
            line = jnp.where(lane // ROWS == i, pbuf[g * 8 + i], line)
        total.append(line)
    line = jnp.concatenate(total, axis=1)
    kpos[0] = line
    qpos[0] = line
    start_all(pos_copies())
    arrived(kbuf.at[0, HALF:OWN * ROWS, :], zk_recv.at[1])
    start_all(k_first(1))
    loop(0, NZ // 2, queries_z)
    k_first_arrived(0)
    start_all(k_second(0))
    loop(NZ // 2, OWN, queries_z)
    arrived(vbuf.at[0, 0:HALF, :], zv_recv.at[0])
    start_all(v_first(0))
    arrived(vbuf.at[0, HALF:OWN * ROWS, :], zv_recv.at[1])
    start_all(v_first(1))
    k_first_arrived(1)
    start_all(k_second(1))
    for quarter in range(4):
        rows = PART if quarter < 3 else PART - ROWS
        arrived(qbuf.at[quarter, 3 * PART:3 * PART + rows, :], zq_recv.at[quarter])
        start_all(q_copies(quarter))
        if quarter == 0:
            v_first_arrived(0)
            start_all(v_second(0))
    arrived(kpos.at[0:7], kp_recv)
    arrived(qpos.at[0:3], qp_recv)
    for dy in range(QB):
        for half in range(2):
            line = qpos[dy, :, half * HALF:(half + 1) * HALF]
            line = jnp.transpose(jnp.broadcast_to(line, (HALF, HALF)))
            qcol[2 * half, group(dy), :] = line[0:PART]
            qcol[2 * half + 1, group(dy), :] = line[PART:]
    v_first_arrived(1)
    start_all(v_second(1))
    k_second_arrived()
    v_second_arrived()

    def tile(quarter):
        queries = qbuf[quarter]
        places = qcol[quarter]
        top = jnp.full((BLOCK, D), NEG, jnp.float32)
        for b in range(KB):
            scores = dot_t(queries[:, D:], kbuf[b, :, 0:D])
            for at in range(0, BLOCK, D):
                side = jnp.where(kpos[b, :, at:at + D] <= places, scores[:, at:at + D], NEG)
                s_buf[:, b * BLOCK + at:b * BLOCK + at + D] = side
                top = jnp.maximum(top, side)
        top = jnp.max(top, axis=1, keepdims=True)
        total = jnp.zeros((BLOCK, D), jnp.float32)
        mass = jnp.zeros((BLOCK, D), jnp.float32)
        for b in range(KB):
            cols = pl.ds(b * BLOCK, BLOCK)
            expo = jnp.exp2((s_buf[:, cols] - top) * (SCALE * LOG2E))
            weighted = expo * dot_t(queries, kbuf[b])
            total = total + (expo[:, :D] + expo[:, D:])
            mass = mass + (weighted[:, :D] + weighted[:, D:])
            p_buf[:, cols] = expo.astype(jnp.bfloat16)
            w_buf[:, cols] = weighted.astype(jnp.bfloat16)
        total = jnp.sum(total, axis=1, keepdims=True)
        mass = jnp.sum(mass, axis=1, keepdims=True)
        both = jnp.zeros((BLOCK, 2 * D), jnp.float32)
        third = jnp.zeros((BLOCK, D), jnp.float32)
        for b in range(KB):
            cols = pl.ds(b * BLOCK, BLOCK)
            both = both + jnp.dot(p_buf[:, cols], vbuf[b], preferred_element_type=jnp.float32)
            third = third + jnp.dot(w_buf[:, cols], vbuf[b, :, 0:D], preferred_element_type=jnp.float32)
        inverse = 1.0 / total
        mean = mass * (SCALE * inverse)
        mixed = both[:, :D] * inverse
        tangent = (third * SCALE + both[:, D:]) * inverse - mean * mixed
        lanes = lax.broadcasted_iota(jnp.int32, (BLOCK, D), 1)
        stats = jnp.where(lanes == 0, top * (SCALE * LOG2E), jnp.where(lanes == 1, total, mean))
        part[quarter, :, 0:D] = mixed.astype(jnp.bfloat16)
        part[quarter, :, D:] = tangent.astype(jnp.bfloat16)
        for at in range(2):
            pstat[quarter * 2 + at] = jnp.transpose(stats[at * HALF:(at + 1) * HALF])[0:8]

    def o_copy(quarter, dy):
        return send(part.at[quarter, group(dy), :], opart.at[quarter, group(dy), :],
                    o_send, o_recv.at[quarter], along_y(dy))

    def st_copy(quarter, dy):
        return send(pstat.at[quarter * 2 + DISTANCES.index(dy) // 2], ostat.at[quarter * 4 + dy],
                    st_send, st_recv.at[quarter], along_y(dy))

    def f_copy(i):
        slot = pl.ds(pl.multiple_of(i * ROWS, ROWS), ROWS)
        return send(obuf.at[slot, :], rbuf.at[i], f_send, f_recv, along_z(offset(i)))

    def merge(quarter):
        arrived(part.at[quarter, 0:3 * PART, :], o_recv.at[quarter])
        arrived(pstat.at[0:3], st_recv.at[quarter])
        lines = []
        for dy in range(QB):
            line = pstat[quarter * 2 + 1] if dy == 0 else ostat[quarter * 4 + dy]
            lines.append(pltpu.roll(line, PART, 1) if DISTANCES.index(dy) % 2 else line)
        tops = [line[0:1] for line in lines]
        top = jnp.maximum(jnp.maximum(tops[0], tops[1]), jnp.maximum(tops[2], tops[3]))
        shares = [line[1:2] * jnp.exp2(line[0:1] - top) for line in lines]
        inverse = 1.0 / (shares[0] + shares[1] + shares[2] + shares[3])
        shares = [share * inverse for share in shares]
        mean = sum(share * line[2:3] for share, line in zip(shares, lines))
        shifts = [share * (line[2:3] - mean) for share, line in zip(shares, lines)]
        table = jnp.concatenate(shares + shifts + [jnp.zeros((D - 8, HALF), jnp.float32)], axis=0)
        table = jnp.transpose(table)
        table = table[0:PART]
        mixed = jnp.zeros((PART, D), jnp.float32)
        tangent = jnp.zeros((PART, D), jnp.float32)
        for dy in range(QB):
            held = part if dy == 0 else opart
            one = held[quarter, group(dy), 0:D].astype(jnp.float32)
            two = held[quarter, group(dy), D:].astype(jnp.float32)
            mixed = mixed + table[:, dy:dy + 1] * one
            tangent = tangent + (table[:, dy:dy + 1] * two + table[:, 4 + dy:5 + dy] * one)
        rows = pl.ds(pl.multiple_of(quarter * PART, PART), PART)
        obuf[rows, 0:D] = mixed.astype(jnp.bfloat16)
        obuf[rows, D:] = tangent.astype(jnp.bfloat16)

        def f_start(i):
            @pl.when(i < OWN)
            def _():
                f_copy(i).start()

        loop(quarter * SLOTS, (quarter + 1) * SLOTS, f_start)

    def step(i):
        @pl.when(i < 4)
        def _():
            arrived(qbuf.at[i, 0:3 * PART, :], q_recv.at[i])
            tile(i)
            for dy in (2, 1, 3):
                o_copy(i, dy).start()
                st_copy(i, dy).start()

        @pl.when(i >= 2)
        def _():
            merge(i - 2)

    loop(0, 6, step)

    loop(0, OWN, lambda i: zq(i).wait_send())
    arrived(pbuf.at[0:OWN], zp_send)
    arrived(kpos.at[0:7], kp_send)
    arrived(qpos.at[0:3], qp_send)
    k_left()
    v_left()
    arrived(qbuf.at[:, 0:3 * PART, :], q_send)
    arrived(part.at[:, 0:3 * PART, :], o_send)
    arrived(ostat.at[0:12], st_send)

    def place(head, held):
        cols = pl.ds(pl.multiple_of(head * D, D), D)
        out_ref[:, cols] = held[:, 0:D]
        tan_ref[:, cols] = held[:, D:]

    place(z, obuf[OWN * ROWS:, :])

    def finish(i):
        place((z - offset(i) + NZ) % NZ, rbuf[i])

    arrived(rbuf.at[0:OWN], f_recv)
    loop(0, OWN, finish)
    arrived(rbuf.at[0:OWN], f_send)


def local(*args):
    dma = pltpu.SemaphoreType.DMA
    bf16, f32, i32 = jnp.bfloat16, jnp.float32, jnp.int32
    return pl.pallas_call(
        kernel,
        out_shape=(pltpu.VMEM((ROWS, NZ * D), bf16),) * 2,
        in_specs=[pl.BlockSpec(memory_space=pl.ANY)] * 7,
        out_specs=(pl.BlockSpec(memory_space=pltpu.VMEM),) * 2,
        scratch_shapes=[pltpu.VMEM((ROWS, NZ * D), bf16)] * 6 + [
            pltpu.SMEM((ROWS,), i32),
            dma((7,)),
            pltpu.VMEM((BLOCK, 2 * D), bf16),
            pltpu.VMEM((BLOCK, 2 * D), bf16),
            pltpu.VMEM((BLOCK, 2 * D), bf16),
            pltpu.VMEM((1, D), i32),
            pltpu.VMEM((KB, BLOCK, 2 * D), bf16),
            pltpu.VMEM((KB, BLOCK, 2 * D), bf16),
            pltpu.VMEM((4, BLOCK, 2 * D), bf16),
            pltpu.VMEM((NZ, 1, D), i32),
            pltpu.VMEM((KB, 1, BLOCK), i32),
            pltpu.VMEM((QB, 1, BLOCK), i32),
            pltpu.VMEM((4, BLOCK, D), i32),
            pltpu.VMEM((BLOCK, KB * BLOCK), f32),
            pltpu.VMEM((BLOCK, KB * BLOCK), bf16),
            pltpu.VMEM((BLOCK, KB * BLOCK), bf16),
            pltpu.VMEM((4, BLOCK, 2 * D), bf16),
            pltpu.VMEM((8, 8, HALF), f32),
            pltpu.VMEM((4, BLOCK, 2 * D), bf16),
            pltpu.VMEM((4 * QB, 8, HALF), f32),
            pltpu.VMEM((BLOCK, 2 * D), bf16),
            pltpu.VMEM((NZ, ROWS, 2 * D), bf16),
        ] + [
            dma((NZ,)), dma((2,)), dma((NZ,)), dma((2,)), dma((NZ,)), dma((4,)), dma, dma,
            dma, dma((3,)), dma, dma((3,)), dma, dma((4,)), dma, dma, dma, dma,
            dma, dma((4,)), dma, dma((4,)), dma, dma,
        ],
        compiler_params=pltpu.CompilerParams(
            collective_id=0, has_side_effects=True, vmem_limit_bytes=62 * 2 ** 20),
    )(*args)


def solution(mesh):
    rows = P(("seq", "head"), None)
    return jax.shard_map(
        local,
        mesh=mesh,
        in_specs=(rows,) * 6 + (P(("seq", "head")),),
        out_specs=(rows, rows),
        check_vma=False,
    )
```

time: 69.8 us -> 59.7 us (0.86)
  the two profiles are of different devices: /device:TPU:9 before, /device:TPU:4 now
where the time goes in v3:
time: 59.7 us; the launch traced here: 59.5 us
  Pallas kernels  57.6 us (96%)
  local copies, waits for them, and re-layouts  1.26 us (2%)
  between operations  0.64 us (1%)
    pallas_call x1, Pallas kernels, local(): pl.pallas_call(kernel, out_shape=(pltpu.VMEM((ROWS, NZ * D), bf16),) * 2,...  57.6 us
    unnamed x2, local copies, waits for them, and re-layouts  1.26 us

profile of v3, /device:TPU:4, one launch (start us, length us, event | category | flops | bytes accessed | tf_op | source)
XLA Modules:
  0.0 59.5 jit_solution(5688521798254360172)
XLA Ops:
  0.6 57.6 %shard_map.86 = (bf16[16,2048]{1,0:T(8,128)(2,1)S(1)}, bf16[16,2048]{1,0:T(8,128)(2,1)S(1)}) custom-call(bf16[16,2048]{1,0:T(8,128)(2,1)} %q_hbm.1, bf16[16,2048]{1,0:T(8,128)(2,1)} %k_hbm.1, bf16[16,2048]{1,0:T(8,128)(2,1)} %v_hbm.1, bf16[16,2048]{1,0:T(8,128)(2,1)} %dq_hbm.1, bf16[16,2048]{1,0:T(8,128)(2,1)} %dk_hbm.1, bf16[16,2048]{1,0:T(8,128)(2,1)} %dv_hbm.1, ...), custom_call_target="tpu_custom_call" | custom-call | tf_op jit(solution)/shard_map/pallas_call | solution.py:405
  58.2 0.6 %copy.11 = bf16[16,2048]{1,0:T(8,128)(2,1)} copy(bf16[16,2048]{1,0:T(8,128)(2,1)S(1)} %get-tuple-element.2) | data formatting | bytes 131072
  58.9 0.6 %copy.12 = bf16[16,2048]{1,0:T(8,128)(2,1)} copy(bf16[16,2048]{1,0:T(8,128)(2,1)S(1)} %get-tuple-element.3) | data formatting | bytes 131072

commit v4 on v3

--- a/solution.py
+++ b/solution.py
@@ -90,7 +90,7 @@
     def greet(to):
         pl.semaphore_signal(barrier, inc=1, device_id=to, device_id_type=MESH)
 
-    loop(1, NZ, lambda i: greet(along_z(i)))
+    loop(0, OWN, lambda i: greet(along_z(offset(i))))
     for by in (1, 2, 3):
         greet(along_x(by))
         greet(across_x(by))
@@ -251,13 +251,6 @@
     start_all(v_first(1))
     k_first_arrived(1)
     start_all(k_second(1))
-    for quarter in range(4):
-        rows = PART if quarter < 3 else PART - ROWS
-        arrived(qbuf.at[quarter, 3 * PART:3 * PART + rows, :], zq_recv.at[quarter])
-        start_all(q_copies(quarter))
-        if quarter == 0:
-            v_first_arrived(0)
-            start_all(v_second(0))
     arrived(kpos.at[0:7], kp_recv)
     arrived(qpos.at[0:3], qp_recv)
     for dy in range(QB):
@@ -266,44 +259,52 @@
             line = jnp.transpose(jnp.broadcast_to(line, (HALF, HALF)))
             qcol[2 * half, group(dy), :] = line[0:PART]
             qcol[2 * half + 1, group(dy), :] = line[PART:]
+    for quarter in range(4):
+        rows = PART if quarter < 3 else PART - ROWS
+        arrived(qbuf.at[quarter, 3 * PART:3 * PART + rows, :], zq_recv.at[quarter])
+        start_all(q_copies(quarter))
+        if quarter == 0:
+            v_first_arrived(0)
+            start_all(v_second(0))
     v_first_arrived(1)
     start_all(v_second(1))
     k_second_arrived()
-    v_second_arrived()
-
-    def tile(quarter):
+
+    def score(quarter, side):
         queries = qbuf[quarter]
         places = qcol[quarter]
         top = jnp.full((BLOCK, D), NEG, jnp.float32)
         for b in range(KB):
             scores = dot_t(queries[:, D:], kbuf[b, :, 0:D])
             for at in range(0, BLOCK, D):
-                side = jnp.where(kpos[b, :, at:at + D] <= places, scores[:, at:at + D], NEG)
-                s_buf[:, b * BLOCK + at:b * BLOCK + at + D] = side
-                top = jnp.maximum(top, side)
+                seen = jnp.where(kpos[b, :, at:at + D] <= places, scores[:, at:at + D], NEG)
+                s_buf[:, b * BLOCK + at:b * BLOCK + at + D] = seen
+                top = jnp.maximum(top, seen)
         top = jnp.max(top, axis=1, keepdims=True)
         total = jnp.zeros((BLOCK, D), jnp.float32)
-        mass = jnp.zeros((BLOCK, D), jnp.float32)
         for b in range(KB):
             cols = pl.ds(b * BLOCK, BLOCK)
             expo = jnp.exp2((s_buf[:, cols] - top) * (SCALE * LOG2E))
             weighted = expo * dot_t(queries, kbuf[b])
             total = total + (expo[:, :D] + expo[:, D:])
-            mass = mass + (weighted[:, :D] + weighted[:, D:])
-            p_buf[:, cols] = expo.astype(jnp.bfloat16)
-            w_buf[:, cols] = weighted.astype(jnp.bfloat16)
-        total = jnp.sum(total, axis=1, keepdims=True)
-        mass = jnp.sum(mass, axis=1, keepdims=True)
+            p_buf[side, :, cols] = expo.astype(jnp.bfloat16)
+            w_buf[side, :, cols] = weighted.astype(jnp.bfloat16)
+        return top, jnp.sum(total, axis=1, keepdims=True)
+
+    def mix(quarter, side, top, total):
         both = jnp.zeros((BLOCK, 2 * D), jnp.float32)
-        third = jnp.zeros((BLOCK, D), jnp.float32)
+        third = jnp.zeros((BLOCK, 2 * D), jnp.float32)
+        ones = jnp.ones((BLOCK, D), jnp.bfloat16)
         for b in range(KB):
             cols = pl.ds(b * BLOCK, BLOCK)
-            both = both + jnp.dot(p_buf[:, cols], vbuf[b], preferred_element_type=jnp.float32)
-            third = third + jnp.dot(w_buf[:, cols], vbuf[b, :, 0:D], preferred_element_type=jnp.float32)
+            both = both + jnp.dot(p_buf[side, :, cols], vbuf[b], preferred_element_type=jnp.float32)
+            third = third + jnp.dot(
+                w_buf[side, :, cols], jnp.concatenate([vbuf[b, :, 0:D], ones], axis=1),
+                preferred_element_type=jnp.float32)
         inverse = 1.0 / total
-        mean = mass * (SCALE * inverse)
+        mean = third[:, D:] * (SCALE * inverse)
         mixed = both[:, :D] * inverse
-        tangent = (third * SCALE + both[:, D:]) * inverse - mean * mixed
+        tangent = (third[:, :D] * SCALE + both[:, D:]) * inverse - mean * mixed
         lanes = lax.broadcasted_iota(jnp.int32, (BLOCK, D), 1)
         stats = jnp.where(lanes == 0, top * (SCALE * LOG2E), jnp.where(lanes == 1, total, mean))
         part[quarter, :, 0:D] = mixed.astype(jnp.bfloat16)
@@ -359,20 +360,29 @@
 
         loop(quarter * SLOTS, (quarter + 1) * SLOTS, f_start)
 
-    def step(i):
-        @pl.when(i < 4)
-        def _():
-            arrived(qbuf.at[i, 0:3 * PART, :], q_recv.at[i])
-            tile(i)
-            for dy in (2, 1, 3):
-                o_copy(i, dy).start()
-                st_copy(i, dy).start()
-
-        @pl.when(i >= 2)
-        def _():
-            merge(i - 2)
-
-    loop(0, 6, step)
+    def q_arrived(quarter):
+        arrived(qbuf.at[quarter, 0:3 * PART, :], q_recv.at[quarter])
+
+    def o_start(quarter):
+        for dy in (2, 1, 3):
+            o_copy(quarter, dy).start()
+            st_copy(quarter, dy).start()
+
+    q_arrived(0)
+    held = score(0, 0)
+    v_second_arrived()
+
+    def step(i, held):
+        q_arrived(i + 1)
+        mix(i, i % 2, *held)
+        o_start(i)
+        held = score(i + 1, (i + 1) % 2)
+        return held
+
+    held = lax.fori_loop(0, 3, step, held)
+    mix(3, 1, *held)
+    o_start(3)
+    loop(0, 4, merge)
 
     loop(0, OWN, lambda i: zq(i).wait_send())
     arrived(pbuf.at[0:OWN], zp_send)
@@ -422,8 +432,8 @@
             pltpu.VMEM((QB, 1, BLOCK), i32),
             pltpu.VMEM((4, BLOCK, D), i32),
             pltpu.VMEM((BLOCK, KB * BLOCK), f32),
-            pltpu.VMEM((BLOCK, KB * BLOCK), bf16),
-            pltpu.VMEM((BLOCK, KB * BLOCK), bf16),
+            pltpu.VMEM((2, BLOCK, KB * BLOCK), bf16),
+            pltpu.VMEM((2, BLOCK, KB * BLOCK), bf16),
             pltpu.VMEM((4, BLOCK, 2 * D), bf16),
             pltpu.VMEM((8, 8, HALF), f32),
             pltpu.VMEM((4, BLOCK, 2 * D), bf16),

time: 59.7 us -> 58.1 us (0.973)
  the two profiles are of different devices: /device:TPU:4 before, /device:TPU:2 now
where the time goes in v4:
time: 58.1 us; the launch traced here: 58 us
  Pallas kernels  56.1 us (97%)
  local copies, waits for them, and re-layouts  1.26 us (2%)
  between operations  0.64 us (1%)
    pallas_call x1, Pallas kernels, local(): pl.pallas_call(kernel, out_shape=(pltpu.VMEM((ROWS, NZ * D), bf16),) * 2,...  56.1 us
    unnamed x2, local copies, waits for them, and re-layouts  1.26 us

profile of v4, /device:TPU:2, one launch (start us, length us, event | category | flops | bytes accessed | tf_op | source)
XLA Modules:
  0.0 58.0 jit_solution(2223640249707363190)
XLA Ops:
  0.6 56.1 %shard_map.86 = (bf16[16,2048]{1,0:T(8,128)(2,1)S(1)}, bf16[16,2048]{1,0:T(8,128)(2,1)S(1)}) custom-call(bf16[16,2048]{1,0:T(8,128)(2,1)} %q_hbm.1, bf16[16,2048]{1,0:T(8,128)(2,1)} %k_hbm.1, bf16[16,2048]{1,0:T(8,128)(2,1)} %v_hbm.1, bf16[16,2048]{1,0:T(8,128)(2,1)} %dq_hbm.1, bf16[16,2048]{1,0:T(8,128)(2,1)} %dk_hbm.1, bf16[16,2048]{1,0:T(8,128)(2,1)} %dv_hbm.1, ...), custom_call_target="tpu_custom_call" | custom-call | tf_op jit(solution)/shard_map/pallas_call | solution.py:415
  56.7 0.6 %copy.11 = bf16[16,2048]{1,0:T(8,128)(2,1)} copy(bf16[16,2048]{1,0:T(8,128)(2,1)S(1)} %get-tuple-element.2) | data formatting | bytes 131072
  57.3 0.6 %copy.12 = bf16[16,2048]{1,0:T(8,128)(2,1)} copy(bf16[16,2048]{1,0:T(8,128)(2,1)S(1)} %get-tuple-element.3) | data formatting | bytes 131072

commit v5 on v4

--- a/solution.py
+++ b/solution.py
@@ -11,6 +11,7 @@
 BLOCK = NZ * ROWS
 HALF = BLOCK // 2
 PART = BLOCK // 4
+OTHERS = 3 * PART
 SLOTS = NZ // 4
 KB = 8
 QB = 4
@@ -18,7 +19,7 @@
 LOG2E = 1.4426950408889634
 NEG = -1e30
 MESH = pl.DeviceIdType.MESH
-DISTANCES = (2, 1, 3, 0)
+DISTANCES = (2, 1, 3)
 OWN = NZ - 1
 
 
@@ -42,8 +43,8 @@
 def kernel(q_hbm, k_hbm, v_hbm, dq_hbm, dk_hbm, dv_hbm, pos_hbm,
            out_ref, tan_ref,
            q_ref, k_ref, v_ref, dq_ref, dk_ref, dv_ref, pos_ref, in_sem,
-           kpack, vpack, qpack, prow, kbuf, vbuf, qbuf, pbuf, kpos, qpos, qcol,
-           s_buf, p_buf, w_buf, part, pstat, opart, ostat, obuf, rbuf,
+           kpack, vpack, qpack, prow, kbuf, vbuf, qown, qoth, pbuf, kpos, qpos, owncol, othcol,
+           s_buf, p_buf, w_buf, mine, mstat, part, pstat, opart, ostat, obuf, rbuf,
            zk_send, zk_recv, zv_send, zv_recv, zq_send, zq_recv, zp_send, zp_recv,
            k_send, k_recv, v_send, v_recv, q_send, q_recv,
            kp_send, kp_recv, qp_send, qp_recv,
@@ -126,12 +127,8 @@
         by = offset(i)
         source = pl.ds(pl.multiple_of(((z - by + NZ) % NZ) * ROWS, ROWS), ROWS)
         slot = pl.ds(pl.multiple_of(i * ROWS, ROWS), ROWS)
-        if buf is qbuf:
-            slot = pl.ds(pl.multiple_of(3 * PART + (i % SLOTS) * ROWS, ROWS), ROWS)
-            target = buf.at[i // SLOTS, slot, :]
-        else:
-            target = buf.at[0, slot, :]
-        shared = i // SLOTS if buf is qbuf else i // (NZ // 2)
+        target = buf.at[slot, :] if buf is qown else buf.at[0, slot, :]
+        shared = i // SLOTS if buf is qown else i // (NZ // 2)
         return send(packed.at[source, :], target, send_sem.at[i], recv_sem.at[shared], along_z(-by))
 
     def zk(i):
@@ -141,7 +138,7 @@
         return z_copy(vpack, vbuf, zv_send, zv_recv, i)
 
     def zq(i):
-        return z_copy(qpack, qbuf, zq_send, zq_recv, i)
+        return z_copy(qpack, qown, zq_send, zq_recv, i)
 
     def zp(i):
         return send(prow, pbuf.at[i], zp_send, zp_recv, along_z(-offset(i)))
@@ -181,7 +178,7 @@
         return pl.ds(DISTANCES.index(dy) * PART, PART)
 
     def q_copy(quarter, dy):
-        return send(qbuf.at[quarter, group(0), :], qbuf.at[quarter, group(dy), :],
+        return send(qown.at[quarter * PART:(quarter + 1) * PART, :], qoth.at[quarter, group(dy), :],
                     q_send, q_recv.at[quarter], along_y(4 - dy))
 
     def q_copies(quarter):
@@ -214,18 +211,11 @@
         fetch.wait()
     pack(v_ref, dv_ref, vpack, vbuf.at[0, OWN * ROWS:, :])
 
-    def values_z(i):
-        zk(i).wait_send()
-        zv(i).start()
-
-    def queries_z(i):
-        zv(i).wait_send()
-        zq(i).start()
-
-    loop(0, OWN, values_z)
+    loop(0, OWN, lambda i: zv(i).start())
     for fetch in fetches[5:]:
         fetch.wait()
-    pack(dq_ref, q_ref, qpack, qbuf.at[3, BLOCK - ROWS:, :])
+    pack(dq_ref, q_ref, qpack, qown.at[OWN * ROWS:, :])
+    loop(0, OWN, lambda i: zq(i).start())
     arrived(kbuf.at[0, 0:HALF, :], zk_recv.at[0])
     start_all(k_first(0))
     arrived(pbuf.at[0:OWN], zp_recv)
@@ -241,10 +231,8 @@
     start_all(pos_copies())
     arrived(kbuf.at[0, HALF:OWN * ROWS, :], zk_recv.at[1])
     start_all(k_first(1))
-    loop(0, NZ // 2, queries_z)
     k_first_arrived(0)
     start_all(k_second(0))
-    loop(NZ // 2, OWN, queries_z)
     arrived(vbuf.at[0, 0:HALF, :], zv_recv.at[0])
     start_all(v_first(0))
     arrived(vbuf.at[0, HALF:OWN * ROWS, :], zv_recv.at[1])
@@ -257,11 +245,14 @@
         for half in range(2):
             line = qpos[dy, :, half * HALF:(half + 1) * HALF]
             line = jnp.transpose(jnp.broadcast_to(line, (HALF, HALF)))
-            qcol[2 * half, group(dy), :] = line[0:PART]
-            qcol[2 * half + 1, group(dy), :] = line[PART:]
+            if dy == 0:
+                owncol[half * HALF:(half + 1) * HALF, :] = line
+            else:
+                othcol[2 * half, group(dy), :] = line[0:PART]
+                othcol[2 * half + 1, group(dy), :] = line[PART:]
     for quarter in range(4):
         rows = PART if quarter < 3 else PART - ROWS
-        arrived(qbuf.at[quarter, 3 * PART:3 * PART + rows, :], zq_recv.at[quarter])
+        arrived(qown.at[quarter * PART:quarter * PART + rows, :], zq_recv.at[quarter])
         start_all(q_copies(quarter))
         if quarter == 0:
             v_first_arrived(0)
@@ -270,47 +261,50 @@
     start_all(v_second(1))
     k_second_arrived()
 
-    def score(quarter, side):
-        queries = qbuf[quarter]
-        places = qcol[quarter]
-        top = jnp.full((BLOCK, D), NEG, jnp.float32)
+    def score(queries, places, side):
+        rows = queries.shape[0]
+        top = jnp.full((rows, D), NEG, jnp.float32)
         for b in range(KB):
             scores = dot_t(queries[:, D:], kbuf[b, :, 0:D])
             for at in range(0, BLOCK, D):
                 seen = jnp.where(kpos[b, :, at:at + D] <= places, scores[:, at:at + D], NEG)
-                s_buf[:, b * BLOCK + at:b * BLOCK + at + D] = seen
+                s_buf[0:rows, b * BLOCK + at:b * BLOCK + at + D] = seen
                 top = jnp.maximum(top, seen)
         top = jnp.max(top, axis=1, keepdims=True)
-        total = jnp.zeros((BLOCK, D), jnp.float32)
+        total = jnp.zeros((rows, D), jnp.float32)
         for b in range(KB):
             cols = pl.ds(b * BLOCK, BLOCK)
-            expo = jnp.exp2((s_buf[:, cols] - top) * (SCALE * LOG2E))
+            expo = jnp.exp2((s_buf[0:rows, cols] - top) * (SCALE * LOG2E))
             weighted = expo * dot_t(queries, kbuf[b])
             total = total + (expo[:, :D] + expo[:, D:])
-            p_buf[side, :, cols] = expo.astype(jnp.bfloat16)
-            w_buf[side, :, cols] = weighted.astype(jnp.bfloat16)
+            p_buf[side, 0:rows, cols] = expo.astype(jnp.bfloat16)
+            w_buf[side, 0:rows, cols] = weighted.astype(jnp.bfloat16)
         return top, jnp.sum(total, axis=1, keepdims=True)
 
-    def mix(quarter, side, top, total):
-        both = jnp.zeros((BLOCK, 2 * D), jnp.float32)
-        third = jnp.zeros((BLOCK, 2 * D), jnp.float32)
+    def mix(held, stats_held, side, top, total):
+        rows = held.shape[0]
+        both = jnp.zeros((rows, 2 * D), jnp.float32)
+        third = jnp.zeros((rows, 2 * D), jnp.float32)
         ones = jnp.ones((BLOCK, D), jnp.bfloat16)
         for b in range(KB):
             cols = pl.ds(b * BLOCK, BLOCK)
-            both = both + jnp.dot(p_buf[side, :, cols], vbuf[b], preferred_element_type=jnp.float32)
+            both = both + jnp.dot(p_buf[side, 0:rows, cols], vbuf[b], preferred_element_type=jnp.float32)
             third = third + jnp.dot(
-                w_buf[side, :, cols], jnp.concatenate([vbuf[b, :, 0:D], ones], axis=1),
+                w_buf[side, 0:rows, cols], jnp.concatenate([vbuf[b, :, 0:D], ones], axis=1),
                 preferred_element_type=jnp.float32)
         inverse = 1.0 / total
         mean = third[:, D:] * (SCALE * inverse)
         mixed = both[:, :D] * inverse
         tangent = (third[:, :D] * SCALE + both[:, D:]) * inverse - mean * mixed
-        lanes = lax.broadcasted_iota(jnp.int32, (BLOCK, D), 1)
+        lanes = lax.broadcasted_iota(jnp.int32, (rows, D), 1)
         stats = jnp.where(lanes == 0, top * (SCALE * LOG2E), jnp.where(lanes == 1, total, mean))
-        part[quarter, :, 0:D] = mixed.astype(jnp.bfloat16)
-        part[quarter, :, D:] = tangent.astype(jnp.bfloat16)
-        for at in range(2):
-            pstat[quarter * 2 + at] = jnp.transpose(stats[at * HALF:(at + 1) * HALF])[0:8]
+        held[:, 0:D] = mixed.astype(jnp.bfloat16)
+        held[:, D:] = tangent.astype(jnp.bfloat16)
+        stats_held[0] = jnp.transpose(stats[0:D])[0:8]
+        rest = stats[D:]
+        if rows < BLOCK:
+            rest = jnp.concatenate([rest, rest], axis=0)
+        stats_held[1] = jnp.transpose(rest)[0:8]
 
     def o_copy(quarter, dy):
         return send(part.at[quarter, group(dy), :], opart.at[quarter, group(dy), :],
@@ -325,11 +319,12 @@
         return send(obuf.at[slot, :], rbuf.at[i], f_send, f_recv, along_z(offset(i)))
 
     def merge(quarter):
-        arrived(part.at[quarter, 0:3 * PART, :], o_recv.at[quarter])
+        arrived(part.at[quarter], o_recv.at[quarter])
         arrived(pstat.at[0:3], st_recv.at[quarter])
-        lines = []
-        for dy in range(QB):
-            line = pstat[quarter * 2 + 1] if dy == 0 else ostat[quarter * 4 + dy]
+        line = mstat[quarter // 2]
+        lines = [jnp.where(quarter % 2 == 1, pltpu.roll(line, PART, 1), line)]
+        for dy in (1, 2, 3):
+            line = ostat[quarter * 4 + dy]
             lines.append(pltpu.roll(line, PART, 1) if DISTANCES.index(dy) % 2 else line)
         tops = [line[0:1] for line in lines]
         top = jnp.maximum(jnp.maximum(tops[0], tops[1]), jnp.maximum(tops[2], tops[3]))
@@ -341,15 +336,15 @@
         table = jnp.concatenate(shares + shifts + [jnp.zeros((D - 8, HALF), jnp.float32)], axis=0)
         table = jnp.transpose(table)
         table = table[0:PART]
+        rows = pl.ds(pl.multiple_of(quarter * PART, PART), PART)
         mixed = jnp.zeros((PART, D), jnp.float32)
         tangent = jnp.zeros((PART, D), jnp.float32)
         for dy in range(QB):
-            held = part if dy == 0 else opart
-            one = held[quarter, group(dy), 0:D].astype(jnp.float32)
-            two = held[quarter, group(dy), D:].astype(jnp.float32)
+            held = mine.at[rows, :] if dy == 0 else opart.at[quarter, group(dy), :]
+            one = held[:, 0:D].astype(jnp.float32)
+            two = held[:, D:].astype(jnp.float32)
             mixed = mixed + table[:, dy:dy + 1] * one
             tangent = tangent + (table[:, dy:dy + 1] * two + table[:, 4 + dy:5 + dy] * one)
-        rows = pl.ds(pl.multiple_of(quarter * PART, PART), PART)
         obuf[rows, 0:D] = mixed.astype(jnp.bfloat16)
         obuf[rows, D:] = tangent.astype(jnp.bfloat16)
 
@@ -361,43 +356,54 @@
         loop(quarter * SLOTS, (quarter + 1) * SLOTS, f_start)
 
     def q_arrived(quarter):
-        arrived(qbuf.at[quarter, 0:3 * PART, :], q_recv.at[quarter])
+        arrived(qoth.at[quarter], q_recv.at[quarter])
 
     def o_start(quarter):
         for dy in (2, 1, 3):
             o_copy(quarter, dy).start()
             st_copy(quarter, dy).start()
 
+    def other_score(quarter, side):
+        return score(qoth[quarter], othcol[quarter], side)
+
+    def other_mix(quarter, side, held):
+        mix(part.at[quarter], pstat.at[pl.ds(quarter * 2, 2)], side, *held)
+        o_start(quarter)
+
+    kept = score(qown[...], owncol[...], 2)
     q_arrived(0)
-    held = score(0, 0)
+    held = other_score(0, 0)
     v_second_arrived()
 
     def step(i, held):
         q_arrived(i + 1)
-        mix(i, i % 2, *held)
-        o_start(i)
-        held = score(i + 1, (i + 1) % 2)
-        return held
+        other_mix(i, i % 2, held)
+        return other_score(i + 1, (i + 1) % 2)
 
     held = lax.fori_loop(0, 3, step, held)
-    mix(3, 1, *held)
-    o_start(3)
+    mix(mine, mstat, 2, *kept)
+    other_mix(3, 1, held)
     loop(0, 4, merge)
 
-    loop(0, OWN, lambda i: zq(i).wait_send())
+    def waits(i):
+        zk(i).wait_send()
+        zv(i).wait_send()
+        zq(i).wait_send()
+
+    loop(0, OWN, waits)
     arrived(pbuf.at[0:OWN], zp_send)
     arrived(kpos.at[0:7], kp_send)
     arrived(qpos.at[0:3], qp_send)
     k_left()
     v_left()
-    arrived(qbuf.at[:, 0:3 * PART, :], q_send)
-    arrived(part.at[:, 0:3 * PART, :], o_send)
+    arrived(qoth, q_send)
+    arrived(part, o_send)
     arrived(ostat.at[0:12], st_send)
 
     def place(head, held):
         cols = pl.ds(pl.multiple_of(head * D, D), D)
-        out_ref[:, cols] = held[:, 0:D]
-        tan_ref[:, cols] = held[:, D:]
+        out_ref[:, cols] = held[:, 0:D].astype(jnp.float32)
+        tan_ref[:, cols] = held[:, D:].astype(jnp.float32)
 
     place(z, obuf[OWN * ROWS:, :])
 
@@ -409,12 +415,12 @@
     arrived(rbuf.at[0:OWN], f_send)
 
 
-def local(*args):
+def attend(*args):
     dma = pltpu.SemaphoreType.DMA
     bf16, f32, i32 = jnp.bfloat16, jnp.float32, jnp.int32
     return pl.pallas_call(
         kernel,
-        out_shape=(pltpu.VMEM((ROWS, NZ * D), bf16),) * 2,
+        out_shape=(pltpu.VMEM((ROWS, NZ * D), f32),) * 2,
         in_specs=[pl.BlockSpec(memory_space=pl.ANY)] * 7,
         out_specs=(pl.BlockSpec(memory_space=pltpu.VMEM),) * 2,
         scratch_shapes=[pltpu.VMEM((ROWS, NZ * D), bf16)] * 6 + [
@@ -426,17 +432,21 @@
             pltpu.VMEM((1, D), i32),
             pltpu.VMEM((KB, BLOCK, 2 * D), bf16),
             pltpu.VMEM((KB, BLOCK, 2 * D), bf16),
-            pltpu.VMEM((4, BLOCK, 2 * D), bf16),
+            pltpu.VMEM((BLOCK, 2 * D), bf16),
+            pltpu.VMEM((4, OTHERS, 2 * D), bf16),
             pltpu.VMEM((NZ, 1, D), i32),
             pltpu.VMEM((KB, 1, BLOCK), i32),
             pltpu.VMEM((QB, 1, BLOCK), i32),
-            pltpu.VMEM((4, BLOCK, D), i32),
+            pltpu.VMEM((BLOCK, D), i32),
+            pltpu.VMEM((4, OTHERS, D), i32),
             pltpu.VMEM((BLOCK, KB * BLOCK), f32),
-            pltpu.VMEM((2, BLOCK, KB * BLOCK), bf16),
-            pltpu.VMEM((2, BLOCK, KB * BLOCK), bf16),
-            pltpu.VMEM((4, BLOCK, 2 * D), bf16),
+            pltpu.VMEM((3, BLOCK, KB * BLOCK), bf16),
+            pltpu.VMEM((3, BLOCK, KB * BLOCK), bf16),
+            pltpu.VMEM((BLOCK, 2 * D), bf16),
+            pltpu.VMEM((2, 8, HALF), f32),
+            pltpu.VMEM((4, OTHERS, 2 * D), bf16),
             pltpu.VMEM((8, 8, HALF), f32),
-            pltpu.VMEM((4, BLOCK, 2 * D), bf16),
+            pltpu.VMEM((4, OTHERS, 2 * D), bf16),
             pltpu.VMEM((4 * QB, 8, HALF), f32),
             pltpu.VMEM((BLOCK, 2 * D), bf16),
             pltpu.VMEM((NZ, ROWS, 2 * D), bf16),
@@ -450,6 +460,11 @@
     )(*args)
 
 
+def local(*args):
+    mixed, tangent = attend(*args)
+    return mixed.astype(jnp.bfloat16), tangent.astype(jnp.bfloat16)
+
+
 def solution(mesh):
     rows = P(("seq", "head"), None)
     return jax.shard_map(

time: 58.1 us -> 57.4 us (0.988)
  other arithmetic: 0 us -> 1.28 us
  local copies, waits for them, and re-layouts: 1.26 us -> 0 us
  Pallas kernels: 56.1 us -> 55.4 us
    convert_element_type x0 -> x2, other arithmetic: none -> 1.28 us  [local(): return (mixed.astype(jnp.bfloat16), tangent.astype(jnp.bfloat16))]
    unnamed x2 -> x0, local copies, waits for them, and re-layouts: 1.26 us -> none
    pallas_call x1, Pallas kernels: 56.1 us -> 55.4 us  [attend(): pl.pallas_call(kernel, out_shape=(pltpu.VMEM((ROWS, NZ * D), f32),) * 2,...]
where the time goes in v5:
time: 57.4 us; the launch traced here: 57.3 us
  Pallas kernels  55.4 us (97%)
  other arithmetic  1.28 us (2%)
  between operations  0.64 us (1%)
    pallas_call x1, Pallas kernels, attend(): pl.pallas_call(kernel, out_shape=(pltpu.VMEM((ROWS, NZ * D), f32),) * 2,...  55.4 us
    convert_element_type x2, other arithmetic, local(): return (mixed.astype(jnp.bfloat16), tangent.astype(jnp.bfloat16))  1.28 us

profile of v5, /device:TPU:2, one launch (start us, length us, event | category | flops | bytes accessed | tf_op | source)
XLA Modules:
  0.0 57.3 jit_solution(12278394545888483741)
XLA Ops:
  0.6 55.4 %shard_map.86 = (f32[16,2048]{1,0:T(8,128)S(1)}, f32[16,2048]{1,0:T(8,128)S(1)}) custom-call(bf16[16,2048]{1,0:T(8,128)(2,1)} %q_hbm.1, bf16[16,2048]{1,0:T(8,128)(2,1)} %k_hbm.1, bf16[16,2048]{1,0:T(8,128)(2,1)} %v_hbm.1, bf16[16,2048]{1,0:T(8,128)(2,1)} %dq_hbm.1, bf16[16,2048]{1,0:T(8,128)(2,1)} %dk_hbm.1, bf16[16,2048]{1,0:T(8,128)(2,1)} %dv_hbm.1, ...), custom_call_target="tpu_custom_call" | custom-call | tf_op jit(solution)/shard_map/pallas_call | solution.py:421
  56.0 0.6 %convert_element_type.6 = bf16[16,2048]{1,0:T(8,128)(2,1)} convert(f32[16,2048]{1,0:T(8,128)S(1)} %get-tuple-element.4) | non-fusion elementwise | flops 32768 | bytes 196608 | tf_op jit(solution)/shard_map/convert_element_type | solution.py:465
  56.6 0.6 %convert_element_type.7 = bf16[16,2048]{1,0:T(8,128)(2,1)} convert(f32[16,2048]{1,0:T(8,128)S(1)} %get-tuple-element.5) | non-fusion elementwise | flops 32768 | bytes 196608 | tf_op jit(solution)/shard_map/convert_element_type | solution.py:465

commit v6 on v5

--- a/solution.py
+++ b/solution.py
@@ -41,7 +41,7 @@
 
 
 def kernel(q_hbm, k_hbm, v_hbm, dq_hbm, dk_hbm, dv_hbm, pos_hbm,
-           out_ref, tan_ref,
+           out_ref,
            q_ref, k_ref, v_ref, dq_ref, dk_ref, dv_ref, pos_ref, in_sem,
            kpack, vpack, qpack, prow, kbuf, vbuf, qown, qoth, pbuf, kpos, qpos, owncol, othcol,
            s_buf, p_buf, w_buf, mine, mstat, part, pstat, opart, ostat, obuf, rbuf,
@@ -402,8 +402,8 @@
 
     def place(head, held):
         cols = pl.ds(pl.multiple_of(head * D, D), D)
-        out_ref[:, cols] = held[:, 0:D].astype(jnp.float32)
-        tan_ref[:, cols] = held[:, D:].astype(jnp.float32)
+        out_ref[0, :, cols] = held[:, 0:D]
+        out_ref[1, :, cols] = held[:, D:]
 
     place(z, obuf[OWN * ROWS:, :])
 
@@ -420,9 +420,9 @@
     bf16, f32, i32 = jnp.bfloat16, jnp.float32, jnp.int32
     return pl.pallas_call(
         kernel,
-        out_shape=(pltpu.VMEM((ROWS, NZ * D), f32),) * 2,
+        out_shape=pltpu.VMEM((2, ROWS, NZ * D), bf16),
         in_specs=[pl.BlockSpec(memory_space=pl.ANY)] * 7,
-        out_specs=(pl.BlockSpec(memory_space=pltpu.VMEM),) * 2,
+        out_specs=pl.BlockSpec(memory_space=pltpu.VMEM),
         scratch_shapes=[pltpu.VMEM((ROWS, NZ * D), bf16)] * 6 + [
             pltpu.SMEM((ROWS,), i32),
             dma((7,)),
@@ -461,8 +461,8 @@
 
 
 def local(*args):
-    mixed, tangent = attend(*args)
-    return mixed.astype(jnp.bfloat16), tangent.astype(jnp.bfloat16)
+    both = attend(*args)
+    return both[0], both[1]
 
 
 def solution(mesh):

time: 57.4 us -> 56.8 us (0.990)
  other arithmetic: 1.28 us -> 0 us
  local copies, waits for them, and re-layouts: 0 us -> 0.66 us
    convert_element_type x2 -> x0, other arithmetic: 1.28 us -> none  [local(): return (mixed.astype(jnp.bfloat16), tangent.astype(jnp.bfloat16))]
    squeeze x0 -> x1, local copies, waits for them, and re-layouts: none -> 0.66 us  [local(): return (both[0], both[1])]
where the time goes in v6:
time: 56.8 us; the launch traced here: 56.7 us
  Pallas kernels  55.4 us (98%)
  local copies, waits for them, and re-layouts  0.66 us (1%)
  between operations  0.64 us (1%)
    pallas_call x1, Pallas kernels, attend(): pl.pallas_call(kernel, out_shape=pltpu.VMEM((2, ROWS, NZ * D), bf16), in_...  55.4 us

profile of v6, /device:TPU:2, one launch (start us, length us, event | category | flops | bytes accessed | tf_op | source)
XLA Modules:
  0.0 56.7 jit_solution(1362044175066357904)
XLA Ops:
  0.6 55.4 %shard_map.86 = bf16[2,16,2048]{2,1,0:T(8,128)(2,1)S(1)} custom-call(bf16[16,2048]{1,0:T(8,128)(2,1)} %q_hbm.1, bf16[16,2048]{1,0:T(8,128)(2,1)} %k_hbm.1, bf16[16,2048]{1,0:T(8,128)(2,1)} %v_hbm.1, bf16[16,2048]{1,0:T(8,128)(2,1)} %dq_hbm.1, bf16[16,2048]{1,0:T(8,128)(2,1)} %dk_hbm.1, bf16[16,2048]{1,0:T(8,128)(2,1)} %dv_hbm.1, s32[16]{0:T(128)} %pos_hbm.1), custom_call_target="tpu_custom_call" | custom-call | tf_op jit(solution)/shard_map/pallas_call | solution.py:421
  56.0 0.7 %slice_bitcast_fusion = (bf16[16,2048]{1,0:T(8,128)(2,1)}, bf16[16,2048]{1,0:T(8,128)(2,1)}) fusion(bf16[2,16,2048]{2,1,0:T(8,128)(2,1)S(1)} %shard_map.86), kind=kLoop, calls=%fused_computation | loop fusion | bytes 262144 | tf_op jit(solution)/shard_map/squeeze | solution.py:465
